TPU v7x, 32 devices: a whole 2x2x4 slice. The times are simulated.
32 devices in a mesh: sec: 16 (over z, x, core), env: 2 (over y).
Axes of the slice: x: 2, y: 2, z: 4, core: 2. Of those that a mesh axis runs over, the one named last changes fastest.
Arguments:
- left_env: bfloat16 [1024, 10, 1024], P('sec'), may hold values from -0.1875 to 0.1875
- left_site: bfloat16 [16384, 4, 1024], P('sec', None, 'env'), may hold values from -6 to 6
- bond_vec: float32 [16384], P(('sec', 'env')), may hold values from 0.25 to 4
- right_site: bfloat16 [16384, 4, 1024], P('sec', None, 'env'), may hold values from -0.1875 to 0.1875
- right_env: bfloat16 [16384, 10, 1024], P('sec', None, 'env'), may hold values from -0.0625 to 0.0625
- mpo: float32 [200, 1600], replicated, may hold values from -1 to 1
- bond_profile: int32 [200], replicated, may hold values from 256 to 1024, as said below
- lengths: int32 [16], P('sec'), may hold values from 1 to 16, 200 in all
Outputs:
- junction_out: bfloat16 [1024, 4, 4, 1024], P('sec')
Inputs may be any that keep to these rules, and one draw needn't show every extreme that they name: `bond_profile`: every entry is at least 256 and at most 1024; both ends are taken in every draw. The lengths sum to 200; the longest section has exactly 16 sites.
All inputs are finite; a program needn't handle non-finite values. No bound on the sum of `lengths` on one device may be relied on, other than what follows from the above.
Results may differ from a plain program's by a relative error of at most 0.007.
Values may be sent and summed in bfloat16 or wider, within the bound.
A program may use at most 128 MiB of HBM per device.

v0:
```python
import jax
import jax.numpy as jnp
from jax import lax
from jax.sharding import PartitionSpec as P


def entering(part, axis, combine, identity):
    place = lax.axis_index(axis)
    gathered = lax.all_gather(part, axis)
    state = jnp.zeros_like(part) + jnp.asarray(identity, part.dtype)

    def one(hop, state):
        return combine(state, lax.dynamic_index_in_dim(gathered, hop, 0, False))

    return lax.fori_loop(0, place, one, state)


def shifted(value, axis, steps):
    count = lax.axis_size(axis)
    pairs = [(source, (source + steps) % count) for source in range(count)]
    return lax.ppermute(value, axis, pairs)


def add_counts(earlier, later):
    return earlier + later


def body(left_env, left_site, bond_vec, right_site, right_env, mpo, bond_profile, lengths):
    block_width = left_site.shape[2]
    bond_width = left_site.shape[0]
    site_count = mpo.shape[0]
    mpo_bond = left_env.shape[1]
    local_dim = left_site.shape[1]
    section_start = entering(lengths, "sec", add_counts, jnp.zeros_like(lengths))[0]
    column_ids = lax.axis_index("env") * block_width + jnp.arange(block_width, dtype=jnp.int32)
    bond_ids = jnp.arange(bond_width, dtype=jnp.int32)
    own_site = section_start + lengths[0] - 1
    left_live = bond_profile[(own_site - 1) % site_count]
    middle_live = bond_profile[own_site]
    keep_left = (bond_ids < left_live)[:, None, None] & (column_ids < middle_live)[None, None, :]
    left_used = jnp.where(keep_left, left_site, jnp.zeros_like(left_site))
    row_part = jnp.einsum("xmy,yuc->xmuc", left_env, left_used, preferred_element_type=jnp.float32)
    row_part = (row_part * bond_vec[None, None, None, :]).astype(jnp.bfloat16)
    site_next, env_next = shifted((right_site, right_env), "sec", -1)
    after_site = (own_site + 1) % site_count
    right_live = bond_profile[after_site]
    row_block = lax.all_gather(row_part, "env", axis=3, tiled=True)
    site_used = jnp.where(
        (column_ids < right_live)[None, None, :], site_next, jnp.zeros_like(site_next)
    )
    inner = jnp.einsum("xmuc,cvb->xmuvb", row_block, site_used, preferred_element_type=jnp.float32)
    inner = inner.astype(jnp.bfloat16)
    first_table = lax.dynamic_index_in_dim(mpo, own_site, 0, keepdims=False)
    first_table = first_table.reshape(mpo_bond, mpo_bond, local_dim, local_dim)
    second_table = lax.dynamic_index_in_dim(mpo, after_site, 0, keepdims=False)
    second_table = second_table.reshape(mpo_bond, mpo_bond, local_dim, local_dim)
    mpo_pair = jnp.einsum(
        "mnsu,nktv->msuktv", first_table, second_table, precision=lax.Precision.HIGHEST
    )
    mpo_pair = mpo_pair.astype(jnp.bfloat16)
    mixed = jnp.einsum("xmuvb,msuktv->xstkb", inner, mpo_pair, preferred_element_type=jnp.float32)
    mixed = mixed.astype(jnp.bfloat16)
    env_used = jnp.where((bond_ids < right_live)[:, None, None], env_next, jnp.zeros_like(env_next))
    partial_terms = jnp.einsum(
        "xstkf,bkf->xstb", mixed, env_used, preferred_element_type=jnp.float32
    )
    result = lax.psum(partial_terms, "env").astype(jnp.bfloat16)
    return result


def solution(mesh):
    return jax.shard_map(
        body,
        mesh=mesh,
        in_specs=(
            P("sec", None, None),
            P("sec", None, "env"),
            P(("sec", "env")),
            P("sec", None, "env"),
            P("sec", None, "env"),
            P(),
            P(),
            P("sec"),
        ),
        out_specs=P("sec", None, None, None),
        check_vma=False,
    )
```

profile of v0, /device:TPU:27, one launch (start us, length us, event | category | flops | bytes accessed | tf_op | source)
XLA Modules:
  0.0 351.4 jit_solution(2745066748988065926)
XLA Ops:
  7.3 1.2 dynamic-slice
  8.5 0.7 dynamic-update-slice
  9.2 5.6 %all-reduce = s32[16]{0:T(128)S(1)} all-reduce(s32[16]{0:T(128)S(1)} %dynamic-update-slice), channel_id=2, replica_groups=mesh['sec'=16,'env'=2] {'sec'}, use_global_device_ids=true, to_apply=%add | all-reduce | flops 16 | bytes 128
  14.8 17.4 %while.10 = (s32[]{:T(128)}, s32[1]{0:T(128)}, s32[]{:T(128)}, s32[16,1]{0,1:T(1,128)S(1)}, s32[]{:T(128)}, /*index=5*/s32[]{:T(128)}, s32[]{:T(128)}) while((s32[]{:T(128)}, s32[1]{0:T(128)}, s32[]{:T(128)}, s32[16,1]{0,1:T(1,128)S(1)}, s32[]{:T(128)}, /*index=5*/s32[]{:T(128)}, s32[]{:T(128)}) %tuple.26), condition=%wide.region_1.2_spmd, body=%wide.region_0.1_spmd.sunk | while | flops 6 | bytes 143 | solution.py:15
  16.0 0.6 constant_dynamic-slice_fusion.2
  17.1 0.6 constant_dynamic-slice_fusion.2
  18.3 0.6 constant_dynamic-slice_fusion.2
  19.5 0.6 constant_dynamic-slice_fusion.2
  20.6 0.6 constant_dynamic-slice_fusion.2
  21.8 0.6 constant_dynamic-slice_fusion.2
  23.0 0.6 constant_dynamic-slice_fusion.2
  24.1 0.6 constant_dynamic-slice_fusion.2
  25.3 0.6 constant_dynamic-slice_fusion.2
  32.3 1.5 fusion.29
  33.8 0.6 iota_compare_fusion.1
  34.4 0.7 fusion.27
  35.4 7.8 %select_bitcast_fusion.1 = bf16[1024,4,512,1]{2,1,0,3:T(4,128)(2,1)} fusion(bf16[1024,4,512]{2,1,0:T(4,128)(2,1)} %param.11, pred[1024,512]{1,0:T(8,128)(4,1)S(1)} %broadcast_and_fusion), kind=kLoop, calls=%fused_computation.18 | loop fusion | flops 2097152 | bytes 8912896 | tf_op jit(solution)/shard_map/jit(_where)/select_n | solution.py:41
  43.2 6.4 %fusion.15 = bf16[64,10,4,512]{3,0,1,2:T(8,128)(2,1)} fusion(f32[512]{0:T(512)S(1)} %copy-done.2, bf16[1024,4,512,1]{2,1,0,3:T(4,128)(2,1)} %select_bitcast_fusion.1, bf16[64,10,1024]{2,0,1:T(8,128)(2,1)S(1)} %copy-done), kind=kOutput, calls=%fused_computation.19 | convolution fusion | flops 2686976000 | bytes 8128512 | tf_op jit(solution)/shard_map/xmy,yuc->xmuc/dot_general | solution.py:42
  49.7 2.2 collective-permute-start
  52.1 0.9 dynamic-slice_reduce_fusion
  54.6 0.6 fusion.26
  55.3 0.6 iota_compare_fusion
  55.9 1.8 fusion.23
  57.7 43.0 %collective-permute-done = bf16[1024,4,512]{2,1,0:T(4,128)(2,1)} collective-permute-done((bf16[1024,4,512]{2,1,0:T(4,128)(2,1)}, bf16[1024,4,512]{2,1,0:T(4,128)(2,1)}, u32[]{:S(2)}, u32[]{:S(2)}) %collective-permute-start) | collective-permute-done | bytes 4194336 | tf_op jit(solution)/shard_map/ppermute | solution.py:21
  100.7 5.9 %select_bitcast_fusion = bf16[1024,4,512,1,1]{2,1,0,4,3:T(4,128)(2,1)} fusion(bf16[1024,4,512]{2,1,0:T(4,128)(2,1)} %collective-permute-done, pred[512]{0:T(512)(128)(4,1)S(1)} %fusion.26), kind=kLoop, calls=%fused_computation.17 | loop fusion | flops 2097152 | bytes 8389120 | tf_op jit(solution)/shard_map/jit(_where)/select_n | solution.py:48
  106.5 14.3 %all-gather.3.cloned.1.call-done = bf16[64,10,4,1024]{3,0,1,2:T(8,128)(2,1)} async-done(((bf16[64,10,4,512]{3,0,1,2:T(8,128)(2,1)}), bf16[64,10,4,1024]{3,0,1,2:T(8,128)(2,1)}) %all-gather.3.cloned.1.call-update) | async-done | bytes 5242896 | tf_op jit(solution)/shard_map/all_gather | solution.py:47
  120.8 16.7 %convert_bitcast_fusion = bf16[64,10,4,4,512,1,1]{4,0,3,2,1,6,5:T(8,128)(2,1)} fusion(bf16[1024,4,512,1,1]{2,1,0,4,3:T(4,128)(2,1)} %select_bitcast_fusion, bf16[64,10,4,1024]{3,0,1,2:T(8,128)(2,1)} %all-gather.3.cloned.1.call-done), kind=kOutput, calls=%fused_computation.9 | convolution fusion | flops 10742661120 | bytes 19922944 | tf_op jit(solution)/shard_map/xmuc,cvb->xmuvb/dot_general | solution.py:51
  137.5 54.1 %fusion = bf16[64,4,4,10,512]{4,3,0,2,1:T(8,128)(2,1)} fusion(bf16[64,10,4,4,512,1,1]{4,0,3,2,1,6,5:T(8,128)(2,1)} %convert_bitcast_fusion, bf16[10,4,4,10,4,4,1]{3,0,5,4,2,1,6:T(8,128)(2,1)S(1)} %fusion.23), kind=kOutput, calls=%fused_computation.2 | convolution fusion | flops 1682964480 | bytes 21022720 | tf_op jit(solution)/shard_map/xmuvb,msuktv->xstkb/dot_general | solution.py:61
  191.6 21.4 %collective-permute-done.1 = bf16[1024,10,512]{2,0,1:T(8,128)(2,1)} collective-permute-done((bf16[1024,10,512]{2,0,1:T(8,128)(2,1)}, bf16[1024,10,512]{2,0,1:T(8,128)(2,1)}, u32[]{:S(2)}, u32[]{:S(2)}) %collective-permute-start.1) | collective-permute-done | bytes 10485792 | tf_op jit(solution)/shard_map/ppermute | solution.py:21
  213.0 29.9 %fusion.16 = f32[64,4,4,1024]{3,0,2,1:T(8,128)} fusion(bf16[1024,10,512]{2,0,1:T(8,128)(2,1)} %collective-permute-done.1, pred[1024]{0:T(1024)(128)(4,1)S(1)} %iota_compare_fusion, bf16[64,4,4,10,512]{4,3,0,2,1:T(8,128)(2,1)} %fusion), kind=kOutput, calls=%fused_computation.20 | convolution fusion | flops 10742661120 | bytes 25166848 | tf_op jit(solution)/shard_map/xstkf,bkf->xstb/dot_general | solution.py:64
  242.9 98.3 %all-reduce.2 = bf16[64,4,4,1024]{3,0,2,1:T(8,128)(2,1)S(1)} all-reduce(f32[64,4,4,1024]{3,0,2,1:T(8,128)} %fusion.16), channel_id=1, replica_groups=mesh['sec'=16,'env'=2] {'env'}, use_global_device_ids=true, to_apply=%region_2.3 | all-reduce | flops 1048576 | bytes 6291456 | tf_op jit(solution)/shard_map/psum | solution.py:67
  341.2 2.9 copy.19
  (21 shorter events, 5.7 us)
Async XLA Ops:
  6.5 36.7 %copy-start = (bf16[64,10,1024]{2,0,1:T(8,128)(2,1)S(1)}, bf16[64,10,1024]{2,0,1:T(8,128)(2,1)}, u32[]{:S(2)}) copy-start(bf16[64,10,1024]{2,0,1:T(8,128)(2,1)} %param.10) | copy-start | bytes 3932164
  6.5 114.3 %all-gather.3.cloned.1.call-start = ((), (), s32[]{:S(2)}) async-start(), calls=%async_computation | async-start | bytes 7864320 | tf_op jit(solution)/shard_map/all_gather | solution.py:47
  35.4 7.8 %copy-start.2 = (f32[512]{0:T(512)S(1)}, f32[512]{0:T(512)}, u32[]{:S(2)}) copy-start(f32[512]{0:T(512)} %param.12) | copy-start | bytes 6148
  49.7 51.0 %collective-permute-start = (bf16[1024,4,512]{2,1,0:T(4,128)(2,1)}, bf16[1024,4,512]{2,1,0:T(4,128)(2,1)}, u32[]{:S(2)}, u32[]{:S(2)}) collective-permute-start(bf16[1024,4,512]{2,1,0:T(4,128)(2,1)} %param.13), channel_id=1, source_target_pairs={{0,30},{2,0},{4,2},{6,4},{8,6},{10,8},{12,10},{14,12},{16,14},{18,... | collective-permute-start | bytes 12582920 | tf_op jit(solution)/shard_map/ppermute | solution.py:21
  51.9 161.2 %collective-permute-start.1 = (bf16[1024,10,512]{2,0,1:T(8,128)(2,1)}, bf16[1024,10,512]{2,0,1:T(8,128)(2,1)}, u32[]{:S(2)}, u32[]{:S(2)}) collective-permute-start(bf16[1024,10,512]{2,0,1:T(8,128)(2,1)} %param.14), channel_id=1, source_target_pairs={{0,30},{2,0},{4,2},{6,4},{8,6},{10,8},{12,10},{14,12},{16,14},{18,... | collective-permute-start | bytes 31457288 | tf_op jit(solution)/shard_map/ppermute | solution.py:21
  213.0 131.1 %copy-start.1 = (bf16[64,10,1024]{2,0,1:T(8,128)(2,1)S(1)}, bf16[64,10,1024]{2,0,1:T(8,128)(2,1)}, u32[]{:S(2)}) copy-start(bf16[64,10,1024]{2,0,1:T(8,128)(2,1)} %param.10) | copy-start | bytes 3932164
Sparse Core Ops, SparseCore 0:
  49.8 70.9 all-gather.2
where the time goes:
time: 357 us; the launch traced here: 351 us
  matrix products  109 us (31%)
  blocking collectives  104 us (29%)
  waiting for transfers between devices  78.7 us (22%)
  local copies, waits for them, and re-layouts  17.5 us (5%)
  other arithmetic  16.6 us (5%)
  between operations  14.7 us (4%)
  loops' own time  8.76 us (2%)
    psum x1, blocking collectives, body(): result = lax.psum(partial_terms, 'env').astype(jnp.bfloat16)  98.3 us
    ppermute x2, waiting for transfers between devices, shifted(): return lax.ppermute(value, axis, pairs)  64.4 us
    dot_general x1, matrix products, body(): jnp.einsum('xmuvb,msuktv->xstkb', inner, mpo_pair, preferred_element_type...  54.1 us
    dot_general x1, matrix products, body(): jnp.einsum('xstkf,bkf->xstb', mixed, env_used, preferred_element_type=jnp...  29.9 us
    dot_general x1, matrix products, body(): jnp.einsum('xmuc,cvb->xmuvb', row_block, site_used, preferred_element_typ...  16.7 us
    all_gather x1, waiting for transfers between devices, body(): row_block = lax.all_gather(row_part, 'env', axis=3, tiled=True)  14.3 us
    another operation x1, loops' own time, entering(): return lax.fori_loop(0, place, one, state)  8.76 us
    dynamic_slice x15, local copies, waits for them, and re-layouts, one(): return combine(state, lax.dynamic_index_in_dim(gathered, hop, 0, False))  8.67 us
  transfers between devices with their start and end apart: 3, of which 3 were waited for; matrix products, arithmetic and copies ran while one was open for 23% of the time, Pallas kernels for 0%

commit v1 on v0

v1 whole, which is shorter than its diff:
```python
import functools

import jax
import jax.numpy as jnp
from jax import lax
from jax.experimental import pallas as pl
from jax.experimental.pallas import tpu as pltpu
from jax.sharding import PartitionSpec as P

CHUNKS = 2
GROUP = 8
VMEM_BYTES = 56 * 1024 * 1024


def row_kernel(env_ref, site_ref, scale_ref, out_ref, held):
    state = pl.program_id(0)
    states = pl.num_programs(0)
    rows = env_ref.shape[0]
    part = jnp.dot(env_ref[...], site_ref[0], preferred_element_type=jnp.float32)
    part = part * scale_ref[...]
    for u in range(out_ref.shape[0] // rows):

        @pl.when(state == u)
        def _():
            for at in range(0, part.shape[1], 128):
                held[at // 128, pl.ds(u, rows, stride=out_ref.shape[0] // rows), :] = part[:, at:at + 128]

    @pl.when(state == states - 1)
    def _():
        for at in range(held.shape[0]):
            out_ref[:, at * 128:(at + 1) * 128] = held[at].astype(out_ref.dtype)


def make_rows(env_rows, left_site, scale):
    rows, depth = env_rows.shape
    states, _, width = left_site.shape
    return pl.pallas_call(
        row_kernel,
        grid=(states,),
        in_specs=[
            pl.BlockSpec((rows, depth), lambda u: (0, 0)),
            pl.BlockSpec((1, depth, width), lambda u: (u, 0, 0)),
            pl.BlockSpec((1, width), lambda u: (0, 0)),
        ],
        out_specs=pl.BlockSpec((rows * states, width), lambda u: (0, 0)),
        out_shape=jax.ShapeDtypeStruct((rows * states, width), jnp.bfloat16),
        scratch_shapes=[pltpu.VMEM((width // 128, rows * states, 128), jnp.float32)],
        compiler_params=pltpu.CompilerParams(vmem_limit_bytes=VMEM_BYTES),
        cost_estimate=pl.CostEstimate(
            flops=2 * rows * states * depth * width,
            bytes_accessed=2 * (rows * depth + states * depth * width + rows * states * width),
            transcendentals=0,
        ),
    )(env_rows, left_site, scale)


def apply_kernel(pieces, *refs):
    rows_refs = refs[:pieces]
    site_ref, env_ref, pair_ref, mask_ref, out_ref, mixed, total = refs[pieces:]
    step = pl.program_id(0)
    last = pl.num_programs(0) - 1
    place = lax.axis_index("env")
    states, _, width = site_ref.shape
    block = rows_refs[0].shape[1]
    bonds = mixed.shape[0]
    pairs = pair_ref.shape[0] // bonds
    tall = pair_ref.shape[1] // states

    @pl.when(step == 0)
    def _():
        def group(g, carry):
            base = pl.multiple_of(g * (GROUP * tall), 16)
            parts = []
            for v in range(states):
                term = None
                for r in range(pieces):
                    at = pl.multiple_of(lax.rem(place - r + pieces, pieces) * block, 128)
                    one = jnp.dot(
                        rows_refs[r][pl.ds(base, GROUP * tall), :],
                        site_ref[v, pl.ds(at, block), :],
                        preferred_element_type=jnp.float32,
                    )
                    term = one if term is None else term + one
                parts.append(term * mask_ref[...])
            for i in range(GROUP):
                inner = jnp.concatenate([p[i * tall:(i + 1) * tall] for p in parts], axis=0)
                out = jnp.dot(pair_ref[...], inner.astype(jnp.bfloat16), preferred_element_type=jnp.float32)
                out = out.astype(jnp.bfloat16)
                start = pl.multiple_of((g * GROUP + i) * pairs, 16)
                for k in range(bonds):
                    mixed[k, pl.ds(start, pairs), :] = out[k * pairs:(k + 1) * pairs]
            return carry

        lax.fori_loop(0, mixed.shape[1] // (GROUP * pairs), group, 0)
        total[...] = jnp.zeros_like(total)

    total[...] += lax.dot_general(
        mixed[step], env_ref[0], (((1,), (1,)), ((), ())), preferred_element_type=jnp.float32
    )

    @pl.when(step == last)
    def _():
        out_ref[...] = total[...].astype(out_ref.dtype)


def make_terms(rows_pieces, site, env, pair, mask):
    pieces = len(rows_pieces)
    count, block = rows_pieces[0].shape
    states, depth, width = site.shape
    bonds, outs, _ = env.shape
    tall = bonds * states
    lines = count // tall * states * states
    whole = lambda k: (0, 0)
    return pl.pallas_call(
        functools.partial(apply_kernel, pieces),
        grid=(bonds,),
        in_specs=[pl.BlockSpec((count, block), whole)] * pieces
        + [
            pl.BlockSpec((states, depth, width), lambda k: (0, 0, 0)),
            pl.BlockSpec((1, outs, width), lambda k: (k, 0, 0)),
            pl.BlockSpec(pair.shape, whole),
            pl.BlockSpec(mask.shape, whole),
        ],
        out_specs=pl.BlockSpec((lines, outs), whole),
        out_shape=jax.ShapeDtypeStruct((lines, outs), jnp.bfloat16),
        scratch_shapes=[
            pltpu.VMEM((bonds, lines, width), jnp.bfloat16),
            pltpu.VMEM((lines, outs), jnp.float32),
        ],
        compiler_params=pltpu.CompilerParams(vmem_limit_bytes=VMEM_BYTES),
        cost_estimate=pl.CostEstimate(
            flops=4 * count * depth * states * width + 2 * lines * outs * width * bonds,
            bytes_accessed=2 * (states * depth * width + bonds * outs * width + count * depth + lines * outs),
            transcendentals=0,
        ),
    )(*rows_pieces, site, env, pair, mask)


def hop(value, sections, blocks, sec_step, env_step):
    pairs = [
        (s * blocks + e, (s + sec_step) % sections * blocks + (e + env_step) % blocks)
        for s in range(sections)
        for e in range(blocks)
    ]
    return lax.ppermute(value, ("sec", "env"), pairs)


def body(left_env, left_site, bond_vec, right_site, right_env, mpo, bond_profile, lengths):
    sections, blocks = lax.axis_size("sec"), lax.axis_size("env")
    rows, bonds, width = left_env.shape
    _, states, block = left_site.shape
    sites = mpo.shape[0]
    here = lax.axis_index("sec")
    columns = lax.axis_index("env") * block + jnp.arange(block, dtype=jnp.int32)
    ids = jnp.arange(width, dtype=jnp.int32)

    all_lengths = lax.all_gather(lengths, "sec", tiled=True)
    start = jnp.sum(jnp.where(jnp.arange(sections) < here, all_lengths, 0))
    own = start + lengths[0] - 1
    left_live = bond_profile[(own - 1) % sites]
    middle_live = bond_profile[own % sites]
    out_live = bond_profile[(own + 1) % sites]
    before = (start - 1) % sites
    first = start % sites
    right_live = bond_profile[first]

    left_used = jnp.transpose(left_site, (1, 0, 2))
    env_rows = jnp.where((ids < left_live)[None, None, :], left_env, jnp.zeros_like(left_env))
    env_rows = env_rows.reshape(rows * bonds, width)
    scale = jnp.where(columns < middle_live, bond_vec, 0.0)[None, :]

    step = rows // CHUNKS
    sent = []
    for chunk in range(CHUNKS):
        part = make_rows(env_rows[chunk * step * bonds:(chunk + 1) * step * bonds], left_used, scale)
        sent.append([hop(part, sections, blocks, 1, r) for r in range(blocks)])

    site = jnp.transpose(right_site, (1, 0, 2))
    env = jnp.transpose(right_env, (1, 0, 2))
    mask = (columns < right_live).astype(jnp.float32)[None, :]
    tables = mpo.reshape(sites, -1)
    one = lax.dynamic_index_in_dim(tables, before, 0, False).reshape(bonds, bonds, states, states)
    two = lax.dynamic_index_in_dim(tables, first, 0, False).reshape(bonds, bonds, states, states)
    pair = jnp.einsum("mnsu,nktv->kstvmu", one, two, precision=lax.Precision.HIGHEST)
    pair = pair.reshape(bonds * states * states, -1).astype(jnp.bfloat16)

    keep = (ids < out_live)[None, :]
    results = []
    for chunk in range(CHUNKS):
        terms = make_terms(sent[chunk], site, env, pair, mask)
        back = [hop(terms, sections, blocks, -1, r) for r in range(blocks)]
        total = sum(b.astype(jnp.float32) for b in back)
        results.append(jnp.where(keep, total, 0.0).astype(jnp.bfloat16))
    return jnp.concatenate(results, axis=0).reshape(rows, states, states, width)


def solution(mesh):
    return jax.shard_map(
        body,
        mesh=mesh,
        in_specs=(
            P("sec", None, None),
            P("sec", None, "env"),
            P(("sec", "env")),
            P("sec", None, "env"),
            P("sec", None, "env"),
            P(),
            P(),
            P("sec"),
        ),
        out_specs=P("sec", None, None, None),
        check_vma=False,
    )
```

time: 357 us -> 169 us (0.47)
  the two profiles are of different devices: /device:TPU:27 before, /device:TPU:1 now
where the time goes in v1:
time: 169 us; the launch traced here: 168 us
  Pallas kernels  55.6 us (33%)
  waiting for transfers between devices  52.9 us (31%)
  local copies, waits for them, and re-layouts  27.7 us (16%)
  blocking collectives  10.7 us (6%)
  starting transfers between devices  9.99 us (6%)
  other arithmetic  6.91 us (4%)
  between operations  2.79 us (2%)
  matrix products  1.81 us (1%)
    ppermute x8, waiting for transfers between devices, hop(): return lax.ppermute(value, ('sec', 'env'), pairs)  52.9 us
    pallas_call x2, Pallas kernels, make_terms(): pl.pallas_call(functools.partial(apply_kernel, pieces), grid=(bonds,), in...  44 us
    unnamed x7, local copies, waits for them, and re-layouts  11.9 us
    pallas_call x2, Pallas kernels, make_rows(): pl.pallas_call(row_kernel, grid=(states,), in_specs=[pl.BlockSpec((rows,...  11.5 us
    unnamed x1, blocking collectives  10.7 us
    ppermute x8, starting transfers between devices, hop(): return lax.ppermute(value, ('sec', 'env'), pairs)  9.99 us
    convert_element_type x3, local copies, waits for them, and re-layouts, body(): pair = pair.reshape(bonds * states * states, -1).astype(jnp.bfloat16)  6.47 us
  transfers between devices with their start and end apart: 8, of which 5 were waited for; matrix products, arithmetic and copies ran while one was open for 11% of the time, Pallas kernels for 30%

profile of v1, /device:TPU:1, one launch (start us, length us, event | category | flops | bytes accessed | tf_op | source)
XLA Modules:
  0.0 168.4 jit_solution(6828990352335150106)
XLA Ops:
  0.7 1.3 dynamic-slice
  1.9 0.7 dynamic-update-slice
  2.7 10.7 %all-reduce = s32[16]{0:T(128)S(1)} all-reduce(s32[16]{0:T(128)S(1)} %dynamic-update-slice), channel_id=1, replica_groups=mesh['sec'=16,'env'=2] {'sec'}, use_global_device_ids=true, to_apply=%add | all-reduce | flops 16 | bytes 128
  13.3 0.7 fusion.2
  15.3 1.5 fusion.4
  16.8 0.6 iota_compare_fusion
  17.5 1.4 broadcast_select_fusion
  19.4 1.1 slice.13.env_ref
  20.5 5.0 %copy.32 = bf16[1024,4,512]{2,0,1:T(8,128)(2,1)} copy(bf16[1024,4,512]{2,1,0:T(4,128)(2,1)} %param.9) | data formatting | bytes 8388608 | tf_op args[1]
  25.5 1.2 fusion.1
  26.7 5.8 %shard_map.82 = bf16[1280,512]{1,0:T(8,128)(2,1)} custom-call(bf16[320,1024]{1,0:T(8,128)(2,1)} %slice.13.env_ref, bf16[4,1024,512]{2,1,0:T(8,128)(2,1)} %bitcast.23, f32[1,512]{1,0:T(1,128)} %bitcast.29), custom_call_target="tpu_custom_call" | custom-call | flops 1342177280 | bytes 6160384 | tf_op jit(solution)/shard_map/pallas_call | solution.py:37
  32.5 4.5 %collective-permute-start.1 = (bf16[1280,512]{1,0:T(8,128)(2,1)}, bf16[1280,512]{1,0:T(8,128)(2,1)}, u32[]{:S(2)}, u32[]{:S(2)}) collective-permute-start(bf16[1280,512]{1,0:T(8,128)(2,1)} %shard_map.82), channel_id=1, source_target_pairs={{0,3},{1,2},{2,5},{3,4},{4,7},{5,6},{6,9},{7,8},{8,11},{9,10},{10,... | collective-permute-start | bytes 3932168 | tf_op jit(solution)/shard_map/ppermute | solution.py:145
  37.4 1.1 slice.15.env_ref
  38.5 5.8 %shard_map.84 = bf16[1280,512]{1,0:T(8,128)(2,1)} custom-call(bf16[320,1024]{1,0:T(8,128)(2,1)} %slice.15.env_ref, bf16[4,1024,512]{2,1,0:T(8,128)(2,1)} %bitcast.24, f32[1,512]{1,0:T(1,128)} %bitcast.30), custom_call_target="tpu_custom_call" | custom-call | flops 1342177280 | bytes 6160384 | tf_op jit(solution)/shard_map/pallas_call | solution.py:37
  44.3 1.1 collective-permute-start.5
  46.3 0.9 dynamic-slice_reduce_fusion
  48.8 1.8 %fusion = bf16[10,4,4,4,10,4]{4,0,5,1,3,2:T(8,128)(2,1)S(1)} fusion(f32[10,10,4,4,1,1]{0,1,5,4,3,2:T(8,128)S(1)} %copy.23, f32[10,10,4,4,1,1]{1,0,3,2,5,4:T(8,128)S(1)} %copy.24), kind=kOutput, calls=%fused_computation.6 | convolution fusion | flops 3097600 | bytes 64000 | tf_op jit(solution)/shard_map/mnsu,nktv->kstvmu/dot_general | solution.py:184
  50.6 4.8 %copy.19 = bf16[10,4,4,4,10,4]{2,1,0,5,4,3:T(4,128)(2,1)S(1)} copy(bf16[10,4,4,4,10,4]{4,0,5,1,3,2:T(8,128)(2,1)S(1)} %fusion) | data formatting | bytes 102400 | tf_op jit(solution)/shard_map/convert_element_type | solution.py:185
  55.4 0.9 convert_element_type.37
  56.4 0.7 copy.20.refs_4_
  57.1 5.0 %copy.31 = bf16[1024,4,512]{2,0,1:T(8,128)(2,1)} copy(bf16[1024,4,512]{2,1,0:T(4,128)(2,1)} %param.11) | data formatting | bytes 8388608 | tf_op args[3]
  62.1 1.2 compare_convert_fusion.refs_5_
  63.3 3.3 %collective-permute-done.1.refs_1_ = bf16[1280,512]{1,0:T(8,128)(2,1)} collective-permute-done((bf16[1280,512]{1,0:T(8,128)(2,1)}, bf16[1280,512]{1,0:T(8,128)(2,1)}, u32[]{:S(2)}, u32[]{:S(2)}) %collective-permute-start.1) | collective-permute-done | bytes 1310752 | tf_op jit(solution)/shard_map/ppermute | solution.py:145
  66.6 22.0 %shard_map.83 = bf16[512,1024]{1,0:T(8,128)(2,1)} custom-call(bf16[1280,512]{1,0:T(8,128)(2,1)} %collective-permute-done.refs_0_, bf16[1280,512]{1,0:T(8,128)(2,1)} %collective-permute-done.1.refs_1_, bf16[4,1024,512]{2,1,0:T(8,128)(2,1)} %bitcast.25, bf16[10,1024,512]{2,1,0:T(8,128)(2,1)} %bitcast.31, bf16[160,160]{1,0:T(8,128)(2,1)} %copy.20.refs_4_, ...), custom_call_target="tpu_custom_call" | custom-call | flops 16106127360 | bytes 18350080 | tf_op jit(solution)/shard_map/pallas_call | solution.py:114
  88.6 4.1 %collective-permute-start.3 = (bf16[512,1024]{1,0:T(8,128)(2,1)}, bf16[512,1024]{1,0:T(8,128)(2,1)S(1)}, u32[]{:S(2)}, u32[]{:S(2)}) collective-permute-start(bf16[512,1024]{1,0:T(8,128)(2,1)} %shard_map.83), channel_id=1, source_target_pairs={{0,31},{1,30},{2,1},{3,0},{4,3},{5,2},{6,5},{7,4},{8,7},{9,6},{10,... | collective-permute-start | bytes 3145736 | tf_op jit(solution)/shard_map/ppermute | solution.py:145
  92.8 2.0 %collective-permute-done.5.refs_1_ = bf16[1280,512]{1,0:T(8,128)(2,1)} collective-permute-done((bf16[1280,512]{1,0:T(8,128)(2,1)}, bf16[1280,512]{1,0:T(8,128)(2,1)}, u32[]{:S(2)}, u32[]{:S(2)}) %collective-permute-start.5) | collective-permute-done | bytes 1310752 | tf_op jit(solution)/shard_map/ppermute | solution.py:145
  94.8 21.7 %collective-permute-done.4.refs_0_ = bf16[1280,512]{1,0:T(8,128)(2,1)} collective-permute-done((bf16[1280,512]{1,0:T(8,128)(2,1)}, bf16[1280,512]{1,0:T(8,128)(2,1)}, u32[]{:S(2)}, u32[]{:S(2)}) %collective-permute-start.4) | collective-permute-done | bytes 1310752 | tf_op jit(solution)/shard_map/ppermute | solution.py:145
  116.5 22.0 %shard_map.85 = bf16[512,1024]{1,0:T(8,128)(2,1)} custom-call(bf16[1280,512]{1,0:T(8,128)(2,1)} %collective-permute-done.4.refs_0_, bf16[1280,512]{1,0:T(8,128)(2,1)} %collective-permute-done.5.refs_1_, bf16[4,1024,512]{2,1,0:T(8,128)(2,1)} %bitcast.26, bf16[10,1024,512]{2,1,0:T(8,128)(2,1)} %bitcast.32, bf16[160,160]{1,0:T(8,128)(2,1)} %copy.20.refs_4_, ...), custom_call_target="tpu_custom_call" | custom-call | flops 16106127360 | bytes 18350080 | tf_op jit(solution)/shard_map/pallas_call | solution.py:114
  139.1 22.7 %collective-permute-done.7 = bf16[512,1024]{1,0:T(8,128)(2,1)S(1)} collective-permute-done((bf16[512,1024]{1,0:T(8,128)(2,1)}, bf16[512,1024]{1,0:T(8,128)(2,1)S(1)}, u32[]{:S(2)}, u32[]{:S(2)}) %collective-permute-start.7) | collective-permute-done | bytes 1048608 | tf_op jit(solution)/shard_map/ppermute | solution.py:145
  161.8 3.2 %collective-permute-done.6 = bf16[512,1024]{1,0:T(8,128)(2,1)S(1)} collective-permute-done((bf16[512,1024]{1,0:T(8,128)(2,1)}, bf16[512,1024]{1,0:T(8,128)(2,1)S(1)}, u32[]{:S(2)}, u32[]{:S(2)}) %collective-permute-start.6) | collective-permute-done | bytes 1048608 | tf_op jit(solution)/shard_map/ppermute | solution.py:145
  165.0 1.0 select_convert_fusion.1
  166.2 2.2 %reshape.39 = bf16[64,4,4,1024]{3,2,1,0:T(4,128)(2,1)} reshape(bf16[1024,1024]{1,0:T(8,128)(2,1)S(1)} %pad_maximum_fusion) | data formatting | bytes 4194304 | tf_op jit(solution)/shard_map/reshape | solution.py:194
  (20 shorter events, 3.5 us)
Async XLA Ops:
  20.5 5.0 %copy-start = (f32[512]{0:T(512)S(1)}, f32[512]{0:T(512)}, u32[]{:S(2)}) copy-start(f32[512]{0:T(512)} %param.10) | copy-start | bytes 6148
  32.5 34.2 %collective-permute-start.1 = (bf16[1280,512]{1,0:T(8,128)(2,1)}, bf16[1280,512]{1,0:T(8,128)(2,1)}, u32[]{:S(2)}, u32[]{:S(2)}) collective-permute-start(bf16[1280,512]{1,0:T(8,128)(2,1)} %shard_map.82), channel_id=1, source_target_pairs={{0,3},{1,2},{2,5},{3,4},{4,7},{5,6},{6,9},{7,8},{8,11},{9,10},{10,... | collective-permute-start | bytes 3932168 | tf_op jit(solution)/shard_map/ppermute | solution.py:145
  37.0 29.7 %collective-permute-start = (bf16[1280,512]{1,0:T(8,128)(2,1)}, bf16[1280,512]{1,0:T(8,128)(2,1)}, u32[]{:S(2)}, u32[]{:S(2)}) collective-permute-start(bf16[1280,512]{1,0:T(8,128)(2,1)} %shard_map.82), channel_id=1, source_target_pairs={{0,2},{1,3},{2,4},{3,5},{4,6},{5,7},{6,8},{7,9},{8,10},{9,11},{10,... | collective-permute-start | bytes 3932168 | tf_op jit(solution)/shard_map/ppermute | solution.py:145
  44.3 50.5 %collective-permute-start.5 = (bf16[1280,512]{1,0:T(8,128)(2,1)}, bf16[1280,512]{1,0:T(8,128)(2,1)}, u32[]{:S(2)}, u32[]{:S(2)}) collective-permute-start(bf16[1280,512]{1,0:T(8,128)(2,1)} %shard_map.84), channel_id=1, source_target_pairs={{0,3},{1,2},{2,5},{3,4},{4,7},{5,6},{6,9},{7,8},{8,11},{9,10},{10,... | collective-permute-start | bytes 3932168 | tf_op jit(solution)/shard_map/ppermute | solution.py:145
  45.4 71.1 %collective-permute-start.4 = (bf16[1280,512]{1,0:T(8,128)(2,1)}, bf16[1280,512]{1,0:T(8,128)(2,1)}, u32[]{:S(2)}, u32[]{:S(2)}) collective-permute-start(bf16[1280,512]{1,0:T(8,128)(2,1)} %shard_map.84), channel_id=1, source_target_pairs={{0,2},{1,3},{2,4},{3,5},{4,6},{5,7},{6,8},{7,9},{8,10},{9,11},{10,... | collective-permute-start | bytes 3932168 | tf_op jit(solution)/shard_map/ppermute | solution.py:145
  88.6 50.5 %collective-permute-start.3 = (bf16[512,1024]{1,0:T(8,128)(2,1)}, bf16[512,1024]{1,0:T(8,128)(2,1)S(1)}, u32[]{:S(2)}, u32[]{:S(2)}) collective-permute-start(bf16[512,1024]{1,0:T(8,128)(2,1)} %shard_map.83), channel_id=1, source_target_pairs={{0,31},{1,30},{2,1},{3,0},{4,3},{5,2},{6,5},{7,4},{8,7},{9,6},{10,... | collective-permute-start | bytes 3145736 | tf_op jit(solution)/shard_map/ppermute | solution.py:145
  92.8 46.4 %collective-permute-start.2 = (bf16[512,1024]{1,0:T(8,128)(2,1)}, bf16[512,1024]{1,0:T(8,128)(2,1)S(1)}, u32[]{:S(2)}, u32[]{:S(2)}) collective-permute-start(bf16[512,1024]{1,0:T(8,128)(2,1)} %shard_map.83), channel_id=1, source_target_pairs={{0,30},{1,31},{2,0},{3,1},{4,2},{5,3},{6,4},{7,5},{8,6},{9,7},{10,... | collective-permute-start | bytes 3145736 | tf_op jit(solution)/shard_map/ppermute | solution.py:145
  138.5 23.3 %collective-permute-start.7 = (bf16[512,1024]{1,0:T(8,128)(2,1)}, bf16[512,1024]{1,0:T(8,128)(2,1)S(1)}, u32[]{:S(2)}, u32[]{:S(2)}) collective-permute-start(bf16[512,1024]{1,0:T(8,128)(2,1)} %shard_map.85), channel_id=1, source_target_pairs={{0,31},{1,30},{2,1},{3,0},{4,3},{5,2},{6,5},{7,4},{8,7},{9,6},{10,... | collective-permute-start | bytes 3145736 | tf_op jit(solution)/shard_map/ppermute | solution.py:145
  138.5 26.5 %collective-permute-start.6 = (bf16[512,1024]{1,0:T(8,128)(2,1)}, bf16[512,1024]{1,0:T(8,128)(2,1)S(1)}, u32[]{:S(2)}, u32[]{:S(2)}) collective-permute-start(bf16[512,1024]{1,0:T(8,128)(2,1)} %shard_map.85), channel_id=1, source_target_pairs={{0,30},{1,31},{2,0},{3,1},{4,2},{5,3},{6,4},{7,5},{8,6},{9,7},{10,... | collective-permute-start | bytes 3145736 | tf_op jit(solution)/shard_map/ppermute | solution.py:145

commit v2 on v1

--- a/solution.py
+++ b/solution.py
@@ -7,23 +7,82 @@
 from jax.experimental.pallas import tpu as pltpu
 from jax.sharding import PartitionSpec as P
 
-CHUNKS = 2
+CHUNK_PARTS = (1, 2, 1)
 GROUP = 8
 VMEM_BYTES = 56 * 1024 * 1024
 
 
-def row_kernel(env_ref, site_ref, scale_ref, out_ref, held):
+def count_kernel(length_ref, start_ref, slots, send_sem, recv_sem):
+    sections = slots.shape[0]
+    me = lax.axis_index("sec")
+    barrier = pltpu.get_barrier_semaphore()
+    for off in range(1, sections):
+        pl.semaphore_signal(
+            barrier,
+            inc=1,
+            device_id={"sec": lax.rem(me + off, sections)},
+            device_id_type=pl.DeviceIdType.MESH,
+        )
+    pl.semaphore_wait(barrier, sections - 1)
+    copies = []
+    for off in range(1, sections):
+        copy = pltpu.make_async_remote_copy(
+            src_ref=length_ref,
+            dst_ref=slots.at[off],
+            send_sem=send_sem.at[off],
+            recv_sem=recv_sem.at[off],
+            device_id={"sec": lax.rem(me + off, sections)},
+            device_id_type=pl.DeviceIdType.MESH,
+        )
+        copy.start()
+        copies.append(copy)
+    for copy in copies:
+        copy.wait()
+    total = jnp.zeros_like(start_ref)
+    for off in range(1, sections):
+        total = total + slots[off] * (me >= off).astype(jnp.int32)
+    start_ref[...] = total
+
+
+def earlier_sites(lengths, sections):
+    tile = (8, 128)
+    start = pl.pallas_call(
+        count_kernel,
+        in_specs=[pl.BlockSpec(memory_space=pltpu.VMEM)],
+        out_specs=pl.BlockSpec(memory_space=pltpu.VMEM),
+        out_shape=jax.ShapeDtypeStruct(tile, jnp.int32),
+        scratch_shapes=[
+            pltpu.VMEM((sections,) + tile, jnp.int32),
+            pltpu.SemaphoreType.DMA((sections,)),
+            pltpu.SemaphoreType.DMA((sections,)),
+        ],
+        compiler_params=pltpu.CompilerParams(collective_id=0, has_side_effects=True),
+    )(jnp.broadcast_to(lengths[None, :], tile))
+    return start[0, 0]
+
+
+def row_kernel(live_ref, env_ref, site_ref, weight_ref, out_ref, used, held):
     state = pl.program_id(0)
     states = pl.num_programs(0)
-    rows = env_ref.shape[0]
-    part = jnp.dot(env_ref[...], site_ref[0], preferred_element_type=jnp.float32)
-    part = part * scale_ref[...]
-    for u in range(out_ref.shape[0] // rows):
+    rows, depth = env_ref.shape
+    width = weight_ref.shape[1]
+    count = out_ref.shape[0] // rows
+
+    @pl.when(state == 0)
+    def _():
+        ids = lax.broadcasted_iota(jnp.int32, (1, depth), 1)
+        keep = (ids < live_ref[0]).astype(jnp.float32).astype(jnp.bfloat16)
+        used[...] = env_ref[...] * keep
+
+    ids = lax.axis_index("env") * width + lax.broadcasted_iota(jnp.int32, (1, width), 1)
+    scale = jnp.where(ids < live_ref[1], weight_ref[...], 0.0)
+    part = jnp.dot(used[...], site_ref[0], preferred_element_type=jnp.float32) * scale
+    for u in range(count):
 
         @pl.when(state == u)
         def _():
-            for at in range(0, part.shape[1], 128):
-                held[at // 128, pl.ds(u, rows, stride=out_ref.shape[0] // rows), :] = part[:, at:at + 128]
+            for at in range(held.shape[0]):
+                held[at, pl.ds(u, rows, stride=count), :] = part[:, at * 128:(at + 1) * 128]
 
     @pl.when(state == states - 1)
     def _():
@@ -31,27 +90,31 @@
             out_ref[:, at * 128:(at + 1) * 128] = held[at].astype(out_ref.dtype)
 
 
-def make_rows(env_rows, left_site, scale):
+def make_rows(live, env_rows, left_site, weights):
     rows, depth = env_rows.shape
     states, _, width = left_site.shape
     return pl.pallas_call(
         row_kernel,
         grid=(states,),
         in_specs=[
+            pl.BlockSpec(memory_space=pltpu.SMEM),
             pl.BlockSpec((rows, depth), lambda u: (0, 0)),
             pl.BlockSpec((1, depth, width), lambda u: (u, 0, 0)),
             pl.BlockSpec((1, width), lambda u: (0, 0)),
         ],
         out_specs=pl.BlockSpec((rows * states, width), lambda u: (0, 0)),
         out_shape=jax.ShapeDtypeStruct((rows * states, width), jnp.bfloat16),
-        scratch_shapes=[pltpu.VMEM((width // 128, rows * states, 128), jnp.float32)],
+        scratch_shapes=[
+            pltpu.VMEM((rows, depth), jnp.bfloat16),
+            pltpu.VMEM((width // 128, rows * states, 128), jnp.float32),
+        ],
         compiler_params=pltpu.CompilerParams(vmem_limit_bytes=VMEM_BYTES),
         cost_estimate=pl.CostEstimate(
             flops=2 * rows * states * depth * width,
             bytes_accessed=2 * (rows * depth + states * depth * width + rows * states * width),
             transcendentals=0,
         ),
-    )(env_rows, left_site, scale)
+    )(live, env_rows, left_site, weights)
 
 
 def apply_kernel(pieces, *refs):
@@ -150,12 +213,10 @@
     rows, bonds, width = left_env.shape
     _, states, block = left_site.shape
     sites = mpo.shape[0]
-    here = lax.axis_index("sec")
     columns = lax.axis_index("env") * block + jnp.arange(block, dtype=jnp.int32)
     ids = jnp.arange(width, dtype=jnp.int32)
 
-    all_lengths = lax.all_gather(lengths, "sec", tiled=True)
-    start = jnp.sum(jnp.where(jnp.arange(sections) < here, all_lengths, 0))
+    start = earlier_sites(lengths, sections)
     own = start + lengths[0] - 1
     left_live = bond_profile[(own - 1) % sites]
     middle_live = bond_profile[own % sites]
@@ -165,14 +226,16 @@
     right_live = bond_profile[first]
 
     left_used = jnp.transpose(left_site, (1, 0, 2))
-    env_rows = jnp.where((ids < left_live)[None, None, :], left_env, jnp.zeros_like(left_env))
-    env_rows = env_rows.reshape(rows * bonds, width)
-    scale = jnp.where(columns < middle_live, bond_vec, 0.0)[None, :]
-
-    step = rows // CHUNKS
+    live = jnp.stack([left_live, middle_live])
+    weights = bond_vec[None, :]
+
+    cuts = [0]
+    for share in CHUNK_PARTS:
+        cuts.append(cuts[-1] + rows * share // sum(CHUNK_PARTS))
     sent = []
-    for chunk in range(CHUNKS):
-        part = make_rows(env_rows[chunk * step * bonds:(chunk + 1) * step * bonds], left_used, scale)
+    for low, high in zip(cuts[:-1], cuts[1:]):
+        env_rows = left_env[low:high].reshape((high - low) * bonds, width)
+        part = make_rows(live, env_rows, left_used, weights)
         sent.append([hop(part, sections, blocks, 1, r) for r in range(blocks)])
 
     site = jnp.transpose(right_site, (1, 0, 2))
@@ -186,8 +249,8 @@
 
     keep = (ids < out_live)[None, :]
     results = []
-    for chunk in range(CHUNKS):
-        terms = make_terms(sent[chunk], site, env, pair, mask)
+    for pieces in sent:
+        terms = make_terms(pieces, site, env, pair, mask)
         back = [hop(terms, sections, blocks, -1, r) for r in range(blocks)]
         total = sum(b.astype(jnp.float32) for b in back)
         results.append(jnp.where(keep, total, 0.0).astype(jnp.bfloat16))

time: 169 us -> 149 us (0.88)
  waiting for transfers between devices: 52.9 us -> 17 us
  Pallas kernels: 55.6 us -> 79.1 us
  blocking collectives: 10.7 us -> 0 us
  starting transfers between devices: 9.99 us -> 13.6 us
  other arithmetic: 6.91 us -> 4.71 us
    ppermute x8 -> x12, waiting for transfers between devices: 52.9 us -> 17 us  [hop(): return lax.ppermute(value, ('sec', 'env'), pairs)]
    pallas_call x2 -> x4, Pallas kernels: 11.5 us -> 25.3 us  [the longest x3 15.6 us: make_rows(): pl.pallas_call(row_kernel, grid=(states,), in_specs=[pl.BlockSpec(memory_...]
    unnamed x1 -> x0, blocking collectives: 10.7 us -> none
    pallas_call x2 -> x3, Pallas kernels: 44 us -> 53.8 us  [make_terms(): pl.pallas_call(functools.partial(apply_kernel, pieces), grid=(bonds,), in...]
    ppermute x8 -> x12, starting transfers between devices: 9.99 us -> 13.6 us  [hop(): return lax.ppermute(value, ('sec', 'env'), pairs)]
    reshape x0 -> x3, local copies, waits for them, and re-layouts: none -> 2.76 us  [body(): env_rows = left_env[low:high].reshape((high - low) * bonds, width)]
    select_n x2 -> x0, other arithmetic: 2.62 us -> none  [the longest x1 1.41 us: body(): jnp.where((ids < left_live)[None, None, :], left_env, jnp.zeros_like(left...]
    another operation x0 -> x1, other arithmetic: none -> 1.87 us  [body(): live = jnp.stack([left_live, middle_live])]
  transfers between devices with their start and end apart: 8 -> 12, of which waited for: 5 -> 2; matrix products, arithmetic and copies ran while one was open for 11% -> 14% of each run, Pallas kernels for 30% -> 43%
where the time goes in v2:
time: 149 us; the launch traced here: 148 us
  Pallas kernels  79.1 us (53%)
  local copies, waits for them, and re-layouts  29.2 us (20%)
  waiting for transfers between devices  17 us (11%)
  starting transfers between devices  13.6 us (9%)
  other arithmetic  4.71 us (3%)
  between operations  2.59 us (2%)
  matrix products  1.81 us (1%)
    pallas_call x3, Pallas kernels, make_terms(): pl.pallas_call(functools.partial(apply_kernel, pieces), grid=(bonds,), in...  53.8 us
    ppermute x12, waiting for transfers between devices, hop(): return lax.ppermute(value, ('sec', 'env'), pairs)  17 us
    pallas_call x3, Pallas kernels, make_rows(): pl.pallas_call(row_kernel, grid=(states,), in_specs=[pl.BlockSpec(memory_...  15.6 us
    ppermute x12, starting transfers between devices, hop(): return lax.ppermute(value, ('sec', 'env'), pairs)  13.6 us
    unnamed x10, local copies, waits for them, and re-layouts  10.9 us
    pallas_call x1, Pallas kernels, earlier_sites(): pl.pallas_call(count_kernel, in_specs=[pl.BlockSpec(memory_space=pltpu.VM...  9.79 us
    convert_element_type x3, local copies, waits for them, and re-layouts, body(): pair = pair.reshape(bonds * states * states, -1).astype(jnp.bfloat16)  6.48 us
  transfers between devices with their start and end apart: 12, of which 2 were waited for; matrix products, arithmetic and copies ran while one was open for 14% of the time, Pallas kernels for 43%

profile of v2, /device:TPU:1, one launch (start us, length us, event | category | flops | bytes accessed | tf_op | source)
XLA Modules:
  0.0 148.1 jit_solution(17400188233800220984)
XLA Ops:
  1.2 9.8 %shard_map.82 = s32[8,128]{1,0:T(8,128)} custom-call(s32[8,128]{1,0:T(8,128)} %broadcast_in_dim.42.length_ref), custom_call_target="tpu_custom_call" | custom-call | tf_op jit(solution)/shard_map/pallas_call | solution.py:49
  11.0 1.2 slice.12
  13.4 1.1 fusion.1
  14.8 0.8 reshape.40.env_ref
  15.6 5.0 %copy.35 = bf16[1024,4,512]{2,0,1:T(8,128)(2,1)} copy(bf16[1024,4,512]{2,1,0:T(4,128)(2,1)} %param.9) | data formatting | bytes 8388608 | tf_op args[1]
  21.3 1.9 %pad_add_fusion.live_ref = s32[2]{0:T(128)} fusion(s32[1]{0:T(128)} %get-tuple-element.14, s32[1]{0:T(128)} %get-tuple-element.12), kind=kLoop, calls=%fused_computation.12 | loop fusion | flops 2 | bytes 16 | tf_op jit(solution)/shard_map/stack | solution.py:229
  23.2 4.9 %shard_map.83 = bf16[640,512]{1,0:T(8,128)(2,1)} custom-call(s32[2]{0:T(128)} %pad_add_fusion.live_ref, bf16[160,1024]{1,0:T(8,128)(2,1)} %reshape.40.env_ref, bf16[4,1024,512]{2,1,0:T(8,128)(2,1)} %bitcast.22, f32[1,512]{1,0:T(1,128)} %bitcast.30), custom_call_target="tpu_custom_call" | custom-call | flops 671088640 | bytes 5177344 | tf_op jit(solution)/shard_map/pallas_call | solution.py:96
  28.1 2.6 %collective-permute-start.1 = (bf16[640,512]{1,0:T(8,128)(2,1)}, bf16[640,512]{1,0:T(8,128)(2,1)}, u32[]{:S(2)}, u32[]{:S(2)}) collective-permute-start(bf16[640,512]{1,0:T(8,128)(2,1)} %shard_map.83), channel_id=1, source_target_pairs={{0,3},{1,2},{2,5},{3,4},{4,7},{5,6},{6,9},{7,8},{8,11},{9,10},{10,... | collective-permute-start | bytes 1966088 | tf_op jit(solution)/shard_map/ppermute | solution.py:208
  31.3 1.1 reshape.43.env_ref
  32.4 5.8 %shard_map.85 = bf16[1280,512]{1,0:T(8,128)(2,1)} custom-call(s32[2]{0:T(128)} %pad_add_fusion.live_ref, bf16[320,1024]{1,0:T(8,128)(2,1)} %reshape.43.env_ref, bf16[4,1024,512]{2,1,0:T(8,128)(2,1)} %bitcast.23, f32[1,512]{1,0:T(1,128)} %bitcast.31), custom_call_target="tpu_custom_call" | custom-call | flops 1342177280 | bytes 6160384 | tf_op jit(solution)/shard_map/pallas_call | solution.py:96
  38.3 0.7 collective-permute-start.5
  39.6 0.8 reshape.44.env_ref
  40.5 4.8 %shard_map.87 = bf16[640,512]{1,0:T(8,128)(2,1)} custom-call(s32[2]{0:T(128)} %pad_add_fusion.live_ref, bf16[160,1024]{1,0:T(8,128)(2,1)} %reshape.44.env_ref, bf16[4,1024,512]{2,1,0:T(8,128)(2,1)} %bitcast.24, f32[1,512]{1,0:T(1,128)} %bitcast.32), custom_call_target="tpu_custom_call" | custom-call | flops 671088640 | bytes 5177344 | tf_op jit(solution)/shard_map/pallas_call | solution.py:96
  45.3 2.2 %collective-permute-start.9 = (bf16[640,512]{1,0:T(8,128)(2,1)}, bf16[640,512]{1,0:T(8,128)(2,1)S(1)}, u32[]{:S(2)}, u32[]{:S(2)}) collective-permute-start(bf16[640,512]{1,0:T(8,128)(2,1)} %shard_map.87), channel_id=1, source_target_pairs={{0,3},{1,2},{2,5},{3,4},{4,7},{5,6},{6,9},{7,8},{8,11},{9,10},{10,... | collective-permute-start | bytes 1966088 | tf_op jit(solution)/shard_map/ppermute | solution.py:208
  48.0 0.9 dynamic-slice_reduce_fusion
  50.5 1.8 %fusion = bf16[10,4,4,4,10,4]{4,0,5,1,3,2:T(8,128)(2,1)S(1)} fusion(f32[10,10,4,4,1,1]{0,1,5,4,3,2:T(8,128)S(1)} %copy.26, f32[10,10,4,4,1,1]{1,0,3,2,5,4:T(8,128)S(1)} %copy.27), kind=kOutput, calls=%fused_computation.5 | convolution fusion | flops 3097600 | bytes 64000 | tf_op jit(solution)/shard_map/mnsu,nktv->kstvmu/dot_general | solution.py:247
  52.4 4.8 %copy.20 = bf16[10,4,4,4,10,4]{2,1,0,5,4,3:T(4,128)(2,1)S(1)} copy(bf16[10,4,4,4,10,4]{4,0,5,1,3,2:T(8,128)(2,1)S(1)} %fusion) | data formatting | bytes 102400 | tf_op jit(solution)/shard_map/convert_element_type | solution.py:248
  57.1 0.9 convert_element_type.46
  58.1 0.7 copy.21.refs_4_
  58.8 5.1 %copy.34 = bf16[1024,4,512]{2,0,1:T(8,128)(2,1)} copy(bf16[1024,4,512]{2,1,0:T(4,128)(2,1)} %param.11) | data formatting | bytes 8388608 | tf_op args[3]
  63.9 1.2 compare_convert_fusion.refs_5_
  65.8 15.9 %shard_map.84 = bf16[256,1024]{1,0:T(8,128)(2,1)} custom-call(bf16[640,512]{1,0:T(8,128)(2,1)} %collective-permute-done.refs_0_, bf16[640,512]{1,0:T(8,128)(2,1)} %collective-permute-done.1.refs_1_, bf16[4,1024,512]{2,1,0:T(8,128)(2,1)} %bitcast.25, bf16[10,1024,512]{2,1,0:T(8,128)(2,1)} %bitcast.33, bf16[160,160]{1,0:T(8,128)(2,1)} %copy.21.refs_4_, ...), custom_call_target="tpu_custom_call" | custom-call | flops 8053063680 | bytes 16515072 | tf_op jit(solution)/shard_map/pallas_call | solution.py:177
  81.7 3.2 %collective-permute-start.2 = (bf16[256,1024]{1,0:T(8,128)(2,1)}, bf16[256,1024]{1,0:T(8,128)(2,1)S(1)}, u32[]{:S(2)}, u32[]{:S(2)}) collective-permute-start(bf16[256,1024]{1,0:T(8,128)(2,1)} %shard_map.84), channel_id=1, source_target_pairs={{0,30},{1,31},{2,0},{3,1},{4,2},{5,3},{6,4},{7,5},{8,6},{9,7},{10,... | collective-permute-start | bytes 1572872 | tf_op jit(solution)/shard_map/ppermute | solution.py:208
  84.8 22.0 %shard_map.86 = bf16[512,1024]{1,0:T(8,128)(2,1)} custom-call(bf16[1280,512]{1,0:T(8,128)(2,1)} %collective-permute-done.4.refs_0_, bf16[1280,512]{1,0:T(8,128)(2,1)} %collective-permute-done.5.refs_1_, bf16[4,1024,512]{2,1,0:T(8,128)(2,1)} %bitcast.26, bf16[10,1024,512]{2,1,0:T(8,128)(2,1)} %bitcast.34, bf16[160,160]{1,0:T(8,128)(2,1)} %copy.21.refs_4_, ...), custom_call_target="tpu_custom_call" | custom-call | flops 16106127360 | bytes 18350080 | tf_op jit(solution)/shard_map/pallas_call | solution.py:177
  106.9 1.2 collective-permute-start.7
  108.1 1.0 collective-permute-start.6
  109.1 0.8 copy-done.3
  109.9 15.8 %shard_map.88 = bf16[256,1024]{1,0:T(8,128)(2,1)} custom-call(bf16[640,512]{1,0:T(8,128)(2,1)} %copy-done.3, bf16[640,512]{1,0:T(8,128)(2,1)} %copy-done.2, bf16[4,1024,512]{2,1,0:T(8,128)(2,1)} %bitcast.27, bf16[10,1024,512]{2,1,0:T(8,128)(2,1)} %bitcast.35, bf16[160,160]{1,0:T(8,128)(2,1)} %copy.21.refs_4_, f32[1,512]{1,0:T(1,128)} %compare_convert_fusion.refs_5_), custom_call_target="tpu_custom_call" | custom-call | flops 8053063680 | bytes 16515072 | tf_op jit(solution)/shard_map/pallas_call | solution.py:177
  125.8 0.9 collective-permute-start.11
  127.8 14.8 %collective-permute-done.11 = bf16[256,1024]{1,0:T(8,128)(2,1)S(1)} collective-permute-done((bf16[256,1024]{1,0:T(8,128)(2,1)}, bf16[256,1024]{1,0:T(8,128)(2,1)S(1)}, u32[]{:S(2)}, u32[]{:S(2)}) %collective-permute-start.11) | collective-permute-done | bytes 524320 | tf_op jit(solution)/shard_map/ppermute | solution.py:208
  142.6 2.2 %collective-permute-done.10 = bf16[256,1024]{1,0:T(8,128)(2,1)S(1)} collective-permute-done((bf16[256,1024]{1,0:T(8,128)(2,1)}, bf16[256,1024]{1,0:T(8,128)(2,1)S(1)}, u32[]{:S(2)}, u32[]{:S(2)}) %collective-permute-start.10) | collective-permute-done | bytes 524320 | tf_op jit(solution)/shard_map/ppermute | solution.py:208
  145.9 2.2 %reshape.45 = bf16[64,4,4,1024]{3,2,1,0:T(4,128)(2,1)} reshape(bf16[1024,1024]{1,0:T(8,128)(2,1)S(1)} %pad_maximum_fusion) | data formatting | bytes 4194304 | tf_op jit(solution)/shard_map/reshape | solution.py:257
  (37 shorter events, 7.2 us)
Async XLA Ops:
  15.6 5.0 %copy-start.1 = (s32[200]{0:T(256)S(1)}, s32[200]{0:T(256)}, u32[]{:S(2)}) copy-start(s32[200]{0:T(256)} %param.14) | copy-start | bytes 2404
  23.2 7.8 %slice-start = ((bf16[64,10,1024]{2,0,1:T(8,128)(2,1)}), bf16[32,10,1024]{2,0,1:T(8,128)(2,1)S(1)}, s32[]{:S(2)}) async-start(bf16[64,10,1024]{2,0,1:T(8,128)(2,1)} %param.8), calls=%async_computation | async-start | bytes 1310720 | tf_op jit(solution)/shard_map/slice | solution.py:237
  28.1 37.0 %collective-permute-start.1 = (bf16[640,512]{1,0:T(8,128)(2,1)}, bf16[640,512]{1,0:T(8,128)(2,1)}, u32[]{:S(2)}, u32[]{:S(2)}) collective-permute-start(bf16[640,512]{1,0:T(8,128)(2,1)} %shard_map.83), channel_id=1, source_target_pairs={{0,3},{1,2},{2,5},{3,4},{4,7},{5,6},{6,9},{7,8},{8,11},{9,10},{10,... | collective-permute-start | bytes 1966088 | tf_op jit(solution)/shard_map/ppermute | solution.py:208
  30.7 35.1 %collective-permute-start = (bf16[640,512]{1,0:T(8,128)(2,1)}, bf16[640,512]{1,0:T(8,128)(2,1)}, u32[]{:S(2)}, u32[]{:S(2)}) collective-permute-start(bf16[640,512]{1,0:T(8,128)(2,1)} %shard_map.83), channel_id=1, source_target_pairs={{0,2},{1,3},{2,4},{3,5},{4,6},{5,7},{6,8},{7,9},{8,10},{9,11},{10,... | collective-permute-start | bytes 1966088 | tf_op jit(solution)/shard_map/ppermute | solution.py:208
  38.3 43.4 %collective-permute-start.5 = (bf16[1280,512]{1,0:T(8,128)(2,1)}, bf16[1280,512]{1,0:T(8,128)(2,1)}, u32[]{:S(2)}, u32[]{:S(2)}) collective-permute-start(bf16[1280,512]{1,0:T(8,128)(2,1)} %shard_map.85), channel_id=1, source_target_pairs={{0,3},{1,2},{2,5},{3,4},{4,7},{5,6},{6,9},{7,8},{8,11},{9,10},{10,... | collective-permute-start | bytes 3932168 | tf_op jit(solution)/shard_map/ppermute | solution.py:208
  39.0 45.9 %collective-permute-start.4 = (bf16[1280,512]{1,0:T(8,128)(2,1)}, bf16[1280,512]{1,0:T(8,128)(2,1)}, u32[]{:S(2)}, u32[]{:S(2)}) collective-permute-start(bf16[1280,512]{1,0:T(8,128)(2,1)} %shard_map.85), channel_id=1, source_target_pairs={{0,2},{1,3},{2,4},{3,5},{4,6},{5,7},{6,8},{7,9},{8,10},{9,11},{10,... | collective-permute-start | bytes 3932168 | tf_op jit(solution)/shard_map/ppermute | solution.py:208
  45.3 62.8 %collective-permute-start.9 = (bf16[640,512]{1,0:T(8,128)(2,1)}, bf16[640,512]{1,0:T(8,128)(2,1)S(1)}, u32[]{:S(2)}, u32[]{:S(2)}) collective-permute-start(bf16[640,512]{1,0:T(8,128)(2,1)} %shard_map.87), channel_id=1, source_target_pairs={{0,3},{1,2},{2,5},{3,4},{4,7},{5,6},{6,9},{7,8},{8,11},{9,10},{10,... | collective-permute-start | bytes 1966088 | tf_op jit(solution)/shard_map/ppermute | solution.py:208
  58.8 6.2 %copy-start = (bf16[640,512]{1,0:T(8,128)(2,1)S(1)}, bf16[640,512]{1,0:T(8,128)(2,1)}, u32[]{:S(2)}) copy-start(bf16[640,512]{1,0:T(8,128)(2,1)} %shard_map.87) | copy-start | bytes 1966084
  65.1 44.0 %collective-permute-start.8 = (bf16[640,512]{1,0:T(8,128)(2,1)S(1)}, bf16[640,512]{1,0:T(8,128)(2,1)S(1)}, u32[]{:S(2)}, u32[]{:S(2)}) collective-permute-start(bf16[640,512]{1,0:T(8,128)(2,1)S(1)} %copy-done), channel_id=1, source_target_pairs={{0,2},{1,3},{2,4},{3,5},{4,6},{5,7},{6,8},{7,9},{8,10},{9,11},{10,... | collective-permute-start | bytes 1966088 | tf_op jit(solution)/shard_map/ppermute | solution.py:208
  81.7 45.1 %collective-permute-start.3 = (bf16[256,1024]{1,0:T(8,128)(2,1)}, bf16[256,1024]{1,0:T(8,128)(2,1)S(1)}, u32[]{:S(2)}, u32[]{:S(2)}) collective-permute-start(bf16[256,1024]{1,0:T(8,128)(2,1)} %shard_map.84), channel_id=1, source_target_pairs={{0,31},{1,30},{2,1},{3,0},{4,3},{5,2},{6,5},{7,4},{8,7},{9,6},{10,... | collective-permute-start | bytes 1572872 | tf_op jit(solution)/shard_map/ppermute | solution.py:208
  81.7 46.2 %collective-permute-start.2 = (bf16[256,1024]{1,0:T(8,128)(2,1)}, bf16[256,1024]{1,0:T(8,128)(2,1)S(1)}, u32[]{:S(2)}, u32[]{:S(2)}) collective-permute-start(bf16[256,1024]{1,0:T(8,128)(2,1)} %shard_map.84), channel_id=1, source_target_pairs={{0,30},{1,31},{2,0},{3,1},{4,2},{5,3},{6,4},{7,5},{8,6},{9,7},{10,... | collective-permute-start | bytes 1572872 | tf_op jit(solution)/shard_map/ppermute | solution.py:208
  106.9 38.4 %collective-permute-start.7 = (bf16[512,1024]{1,0:T(8,128)(2,1)}, bf16[512,1024]{1,0:T(8,128)(2,1)S(1)}, u32[]{:S(2)}, u32[]{:S(2)}) collective-permute-start(bf16[512,1024]{1,0:T(8,128)(2,1)} %shard_map.86), channel_id=1, source_target_pairs={{0,31},{1,30},{2,1},{3,0},{4,3},{5,2},{6,5},{7,4},{8,7},{9,6},{10,... | collective-permute-start | bytes 3145736 | tf_op jit(solution)/shard_map/ppermute | solution.py:208
  108.1 1.0 copy-start.2
  108.1 37.2 %collective-permute-start.6 = (bf16[512,1024]{1,0:T(8,128)(2,1)}, bf16[512,1024]{1,0:T(8,128)(2,1)S(1)}, u32[]{:S(2)}, u32[]{:S(2)}) collective-permute-start(bf16[512,1024]{1,0:T(8,128)(2,1)} %shard_map.86), channel_id=1, source_target_pairs={{0,30},{1,31},{2,0},{3,1},{4,2},{5,3},{6,4},{7,5},{8,6},{9,7},{10,... | collective-permute-start | bytes 3145736 | tf_op jit(solution)/shard_map/ppermute | solution.py:208
  109.1 0.8 copy-start.3
  125.8 16.8 %collective-permute-start.11 = (bf16[256,1024]{1,0:T(8,128)(2,1)}, bf16[256,1024]{1,0:T(8,128)(2,1)S(1)}, u32[]{:S(2)}, u32[]{:S(2)}) collective-permute-start(bf16[256,1024]{1,0:T(8,128)(2,1)} %shard_map.88), channel_id=1, source_target_pairs={{0,31},{1,30},{2,1},{3,0},{4,3},{5,2},{6,5},{7,4},{8,7},{9,6},{10,... | collective-permute-start | bytes 1572872 | tf_op jit(solution)/shard_map/ppermute | solution.py:208
  126.7 18.1 %collective-permute-start.10 = (bf16[256,1024]{1,0:T(8,128)(2,1)}, bf16[256,1024]{1,0:T(8,128)(2,1)S(1)}, u32[]{:S(2)}, u32[]{:S(2)}) collective-permute-start(bf16[256,1024]{1,0:T(8,128)(2,1)} %shard_map.88), channel_id=1, source_target_pairs={{0,30},{1,31},{2,0},{3,1},{4,2},{5,3},{6,4},{7,5},{8,6},{9,7},{10,... | collective-permute-start | bytes 1572872 | tf_op jit(solution)/shard_map/ppermute | solution.py:208

commit v3 on v2

--- a/solution.py
+++ b/solution.py
@@ -2,6 +2,7 @@
 
 import jax
 import jax.numpy as jnp
+import numpy as np
 from jax import lax
 from jax.experimental import pallas as pl
 from jax.experimental.pallas import tpu as pltpu
@@ -58,24 +59,28 @@
         ],
         compiler_params=pltpu.CompilerParams(collective_id=0, has_side_effects=True),
     )(jnp.broadcast_to(lengths[None, :], tile))
-    return start[0, 0]
-
-
-def row_kernel(live_ref, env_ref, site_ref, weight_ref, out_ref, used, held):
+    return start
+
+
+def row_kernel(start_ref, length_ref, profile_ref, env_ref, site_ref, weight_ref, out_ref, used, held):
     state = pl.program_id(0)
     states = pl.num_programs(0)
     rows, depth = env_ref.shape
     width = weight_ref.shape[1]
     count = out_ref.shape[0] // rows
+    sites = profile_ref.shape[0]
+    own = start_ref[0, 0] + length_ref[0] - 1 + sites
+    left_live = profile_ref[lax.rem(own - 1, sites)]
+    middle_live = profile_ref[lax.rem(own, sites)]
 
     @pl.when(state == 0)
     def _():
         ids = lax.broadcasted_iota(jnp.int32, (1, depth), 1)
-        keep = (ids < live_ref[0]).astype(jnp.float32).astype(jnp.bfloat16)
+        keep = (ids < left_live).astype(jnp.float32).astype(jnp.bfloat16)
         used[...] = env_ref[...] * keep
 
     ids = lax.axis_index("env") * width + lax.broadcasted_iota(jnp.int32, (1, width), 1)
-    scale = jnp.where(ids < live_ref[1], weight_ref[...], 0.0)
+    scale = jnp.where(ids < middle_live, weight_ref[...], 0.0)
     part = jnp.dot(used[...], site_ref[0], preferred_element_type=jnp.float32) * scale
     for u in range(count):
 
@@ -90,7 +95,7 @@
             out_ref[:, at * 128:(at + 1) * 128] = held[at].astype(out_ref.dtype)
 
 
-def make_rows(live, env_rows, left_site, weights):
+def make_rows(tables, env_rows, left_site, weights):
     rows, depth = env_rows.shape
     states, _, width = left_site.shape
     return pl.pallas_call(
@@ -98,6 +103,8 @@
         grid=(states,),
         in_specs=[
             pl.BlockSpec(memory_space=pltpu.SMEM),
+            pl.BlockSpec(memory_space=pltpu.SMEM),
+            pl.BlockSpec(memory_space=pltpu.SMEM),
             pl.BlockSpec((rows, depth), lambda u: (0, 0)),
             pl.BlockSpec((1, depth, width), lambda u: (u, 0, 0)),
             pl.BlockSpec((1, width), lambda u: (0, 0)),
@@ -114,12 +121,12 @@
             bytes_accessed=2 * (rows * depth + states * depth * width + rows * states * width),
             transcendentals=0,
         ),
-    )(live, env_rows, left_site, weights)
+    )(*tables, env_rows, left_site, weights)
 
 
 def apply_kernel(pieces, *refs):
     rows_refs = refs[:pieces]
-    site_ref, env_ref, pair_ref, mask_ref, out_ref, mixed, total = refs[pieces:]
+    start_ref, profile_ref, site_ref, env_ref, pair_ref, out_ref, mixed, total = refs[pieces:]
     step = pl.program_id(0)
     last = pl.num_programs(0) - 1
     place = lax.axis_index("env")
@@ -131,6 +138,10 @@
 
     @pl.when(step == 0)
     def _():
+        right_live = profile_ref[lax.rem(start_ref[0, 0], profile_ref.shape[0])]
+        ids = place * width + lax.broadcasted_iota(jnp.int32, (1, width), 1)
+        keep = (ids < right_live).astype(jnp.float32)
+
         def group(g, carry):
             base = pl.multiple_of(g * (GROUP * tall), 16)
             parts = []
@@ -144,7 +155,7 @@
                         preferred_element_type=jnp.float32,
                     )
                     term = one if term is None else term + one
-                parts.append(term * mask_ref[...])
+                parts.append(term * keep)
             for i in range(GROUP):
                 inner = jnp.concatenate([p[i * tall:(i + 1) * tall] for p in parts], axis=0)
                 out = jnp.dot(pair_ref[...], inner.astype(jnp.bfloat16), preferred_element_type=jnp.float32)
@@ -166,7 +177,7 @@
         out_ref[...] = total[...].astype(out_ref.dtype)
 
 
-def make_terms(rows_pieces, site, env, pair, mask):
+def make_terms(rows_pieces, start, profile, site, env, pair):
     pieces = len(rows_pieces)
     count, block = rows_pieces[0].shape
     states, depth, width = site.shape
@@ -179,10 +190,11 @@
         grid=(bonds,),
         in_specs=[pl.BlockSpec((count, block), whole)] * pieces
         + [
+            pl.BlockSpec(memory_space=pltpu.SMEM),
+            pl.BlockSpec(memory_space=pltpu.SMEM),
             pl.BlockSpec((states, depth, width), lambda k: (0, 0, 0)),
             pl.BlockSpec((1, outs, width), lambda k: (k, 0, 0)),
             pl.BlockSpec(pair.shape, whole),
-            pl.BlockSpec(mask.shape, whole),
         ],
         out_specs=pl.BlockSpec((lines, outs), whole),
         out_shape=jax.ShapeDtypeStruct((lines, outs), jnp.bfloat16),
@@ -196,7 +208,44 @@
             bytes_accessed=2 * (states * depth * width + bonds * outs * width + count * depth + lines * outs),
             transcendentals=0,
         ),
-    )(*rows_pieces, site, env, pair, mask)
+    )(*rows_pieces, start, profile, site, env, pair)
+
+
+def pair_kernel(one_ref, two_ref, rows_ref, match_ref, columns_ref, out_ref):
+    product = lax.dot_general(
+        two_ref[...],
+        one_ref[...],
+        (((0,), (0,)), ((), ())),
+        precision=lax.Precision.HIGHEST,
+        preferred_element_type=jnp.float32,
+    ).astype(jnp.bfloat16)
+    total = jnp.zeros(out_ref.shape, jnp.float32)
+    for v in range(rows_ref.shape[0]):
+        picked = jnp.dot(rows_ref[v], product, preferred_element_type=jnp.float32)
+        picked = (picked * match_ref[...]).astype(jnp.bfloat16)
+        total = total + jnp.dot(picked, columns_ref[v], preferred_element_type=jnp.float32)
+    out_ref[...] = total.astype(out_ref.dtype)
+
+
+def make_pair(one, two, bonds, states):
+    size = bonds * states * states
+    at = np.arange(size)
+    outer, middle, inner = at // (states * states), at // states % states, at % states
+    picks, places = [], []
+    for v in range(states):
+        picks.append(((outer * states + inner) * states + v)[:, None] == at[None, :])
+        places.append((v * bonds * states + outer * states + inner)[:, None] == at[None, :])
+    return pl.pallas_call(
+        pair_kernel,
+        out_shape=jax.ShapeDtypeStruct((size, size), jnp.bfloat16),
+        compiler_params=pltpu.CompilerParams(vmem_limit_bytes=VMEM_BYTES),
+    )(
+        one,
+        two,
+        jnp.asarray(np.stack(picks), jnp.bfloat16),
+        jnp.asarray(middle[:, None] == middle[None, :], jnp.float32),
+        jnp.asarray(np.stack(places), jnp.bfloat16),
+    )
 
 
 def hop(value, sections, blocks, sec_step, env_step):
@@ -213,20 +262,11 @@
     rows, bonds, width = left_env.shape
     _, states, block = left_site.shape
     sites = mpo.shape[0]
-    columns = lax.axis_index("env") * block + jnp.arange(block, dtype=jnp.int32)
     ids = jnp.arange(width, dtype=jnp.int32)
 
     start = earlier_sites(lengths, sections)
-    own = start + lengths[0] - 1
-    left_live = bond_profile[(own - 1) % sites]
-    middle_live = bond_profile[own % sites]
-    out_live = bond_profile[(own + 1) % sites]
-    before = (start - 1) % sites
-    first = start % sites
-    right_live = bond_profile[first]
-
     left_used = jnp.transpose(left_site, (1, 0, 2))
-    live = jnp.stack([left_live, middle_live])
+    small = (start, lengths, bond_profile)
     weights = bond_vec[None, :]
 
     cuts = [0]
@@ -235,22 +275,22 @@
     sent = []
     for low, high in zip(cuts[:-1], cuts[1:]):
         env_rows = left_env[low:high].reshape((high - low) * bonds, width)
-        part = make_rows(live, env_rows, left_used, weights)
+        part = make_rows(small, env_rows, left_used, weights)
         sent.append([hop(part, sections, blocks, 1, r) for r in range(blocks)])
 
     site = jnp.transpose(right_site, (1, 0, 2))
     env = jnp.transpose(right_env, (1, 0, 2))
-    mask = (columns < right_live).astype(jnp.float32)[None, :]
-    tables = mpo.reshape(sites, -1)
-    one = lax.dynamic_index_in_dim(tables, before, 0, False).reshape(bonds, bonds, states, states)
-    two = lax.dynamic_index_in_dim(tables, first, 0, False).reshape(bonds, bonds, states, states)
-    pair = jnp.einsum("mnsu,nktv->kstvmu", one, two, precision=lax.Precision.HIGHEST)
-    pair = pair.reshape(bonds * states * states, -1).astype(jnp.bfloat16)
+    origin = start[0, 0]
+    out_live = bond_profile[(origin + lengths[0]) % sites]
+    one = lax.dynamic_index_in_dim(mpo, (origin - 1) % sites, 0, False)
+    one = one.reshape(bonds, bonds, states * states).transpose(1, 0, 2).reshape(bonds, -1)
+    two = lax.dynamic_index_in_dim(mpo, origin % sites, 0, False).reshape(bonds, -1)
+    pair = make_pair(one, two, bonds, states)
 
     keep = (ids < out_live)[None, :]
     results = []
     for pieces in sent:
-        terms = make_terms(pieces, site, env, pair, mask)
+        terms = make_terms(pieces, start, bond_profile, site, env, pair)
         back = [hop(terms, sections, blocks, -1, r) for r in range(blocks)]
         total = sum(b.astype(jnp.float32) for b in back)
         results.append(jnp.where(keep, total, 0.0).astype(jnp.bfloat16))

time: 149 us -> 142 us (0.953)
  local copies, waits for them, and re-layouts: 29.2 us -> 23.6 us
  Pallas kernels: 79.1 us -> 82.2 us
  other arithmetic: 4.71 us -> 2.86 us
  matrix products: 1.81 us -> 0 us
    convert_element_type x3 -> x0, local copies, waits for them, and re-layouts: 6.48 us -> none  [body(): pair = pair.reshape(bonds * states * states, -1).astype(jnp.bfloat16)]
    pallas_call x0 -> x1, Pallas kernels: none -> 2.84 us  [make_pair(): pl.pallas_call(pair_kernel, out_shape=jax.ShapeDtypeStruct((size, size),...]
    another operation x1 -> x0, other arithmetic: 1.87 us -> none  [body(): live = jnp.stack([left_live, middle_live])]
    dot_general x1 -> x0, matrix products: 1.81 us -> none  [body(): jnp.einsum('mnsu,nktv->kstvmu', one, two, precision=lax.Precision.HIGHEST)]
    unnamed x10 -> x12, local copies, waits for them, and re-layouts: 10.9 us -> 11.8 us
  transfers between devices with their start and end apart: 12 -> 12, of which waited for: 2 -> 2; matrix products, arithmetic and copies ran while one was open for 14% -> 10% of each run, Pallas kernels for 43% -> 48%
where the time goes in v3:
time: 142 us; the launch traced here: 141 us
  Pallas kernels  82.2 us (58%)
  local copies, waits for them, and re-layouts  23.6 us (17%)
  waiting for transfers between devices  15.7 us (11%)
  starting transfers between devices  13.6 us (10%)
  between operations  2.94 us (2%)
  other arithmetic  2.86 us (2%)
    pallas_call x3, Pallas kernels, make_terms(): pl.pallas_call(functools.partial(apply_kernel, pieces), grid=(bonds,), in...  54 us
    ppermute x12, waiting for transfers between devices, hop(): return lax.ppermute(value, ('sec', 'env'), pairs)  15.7 us
    pallas_call x3, Pallas kernels, make_rows(): pl.pallas_call(row_kernel, grid=(states,), in_specs=[pl.BlockSpec(memory_...  15.6 us
    ppermute x12, starting transfers between devices, hop(): return lax.ppermute(value, ('sec', 'env'), pairs)  13.6 us
    unnamed x12, local copies, waits for them, and re-layouts  11.8 us
    pallas_call x1, Pallas kernels, earlier_sites(): pl.pallas_call(count_kernel, in_specs=[pl.BlockSpec(memory_space=pltpu.VM...  9.78 us
  transfers between devices with their start and end apart: 12, of which 2 were waited for; matrix products, arithmetic and copies ran while one was open for 10% of the time, Pallas kernels for 48%

profile of v3, /device:TPU:1, one launch (start us, length us, event | category | flops | bytes accessed | tf_op | source)
XLA Modules:
  0.0 140.9 jit_solution(15687471617435753823)
XLA Ops:
  1.2 9.8 %shard_map.109.start_ref.refs_2_ = s32[8,128]{1,0:T(8,128)} custom-call(s32[8,128]{1,0:T(8,128)} %broadcast_in_dim.41.length_ref), custom_call_target="tpu_custom_call" | custom-call | tf_op jit(solution)/shard_map/pallas_call | solution.py:50
  11.0 1.1 fusion
  12.4 0.8 reshape.28.env_ref
  13.2 5.0 %copy.26 = bf16[1024,4,512]{2,0,1:T(8,128)(2,1)} copy(bf16[1024,4,512]{2,1,0:T(4,128)(2,1)} %param.12) | data formatting | bytes 8388608 | tf_op args[1]
  18.2 4.9 %shard_map.110 = bf16[640,512]{1,0:T(8,128)(2,1)} custom-call(s32[8,128]{1,0:T(8,128)} %shard_map.109.start_ref.refs_2_, s32[1]{0:T(128)} %copy.27.length_ref, s32[200]{0:T(256)} %refs_3_.5, bf16[160,1024]{1,0:T(8,128)(2,1)} %reshape.28.env_ref, bf16[4,1024,512]{2,1,0:T(8,128)(2,1)} %bitcast.14, f32[1,512]{1,0:T(1,128)} %bitcast.21), custom_call_target="tpu_custom_call" | custom-call | flops 671088640 | bytes 5177344 | tf_op jit(solution)/shard_map/pallas_call | solution.py:101
  23.1 2.6 %collective-permute-start.1 = (bf16[640,512]{1,0:T(8,128)(2,1)}, bf16[640,512]{1,0:T(8,128)(2,1)S(1)}, u32[]{:S(2)}, u32[]{:S(2)}) collective-permute-start(bf16[640,512]{1,0:T(8,128)(2,1)} %shard_map.110), channel_id=1, source_target_pairs={{0,3},{1,2},{2,5},{3,4},{4,7},{5,6},{6,9},{7,8},{8,11},{9,10},{10,... | collective-permute-start | bytes 1966088 | tf_op jit(solution)/shard_map/ppermute | solution.py:257
  26.4 1.1 reshape.32.env_ref
  27.5 5.9 %shard_map.113 = bf16[1280,512]{1,0:T(8,128)(2,1)} custom-call(s32[8,128]{1,0:T(8,128)} %shard_map.109.start_ref.refs_2_, s32[1]{0:T(128)} %copy.27.length_ref, s32[200]{0:T(256)} %refs_3_.5, bf16[320,1024]{1,0:T(8,128)(2,1)} %reshape.32.env_ref, bf16[4,1024,512]{2,1,0:T(8,128)(2,1)} %bitcast.15, f32[1,512]{1,0:T(1,128)} %bitcast.22), custom_call_target="tpu_custom_call" | custom-call | flops 1342177280 | bytes 6160384 | tf_op jit(solution)/shard_map/pallas_call | solution.py:101
  33.4 0.7 collective-permute-start.5
  34.7 0.9 reshape.33.env_ref
  35.6 4.8 %shard_map.115 = bf16[640,512]{1,0:T(8,128)(2,1)} custom-call(s32[8,128]{1,0:T(8,128)} %shard_map.109.start_ref.refs_2_, s32[1]{0:T(128)} %copy.27.length_ref, s32[200]{0:T(256)} %refs_3_.5, bf16[160,1024]{1,0:T(8,128)(2,1)} %reshape.33.env_ref, bf16[4,1024,512]{2,1,0:T(8,128)(2,1)} %bitcast.16, f32[1,512]{1,0:T(1,128)} %bitcast.23), custom_call_target="tpu_custom_call" | custom-call | flops 671088640 | bytes 5177344 | tf_op jit(solution)/shard_map/pallas_call | solution.py:101
  40.4 2.2 %collective-permute-start.9 = (bf16[640,512]{1,0:T(8,128)(2,1)}, bf16[640,512]{1,0:T(8,128)(2,1)}, u32[]{:S(2)}, u32[]{:S(2)}) collective-permute-start(bf16[640,512]{1,0:T(8,128)(2,1)} %shard_map.115), channel_id=1, source_target_pairs={{0,3},{1,2},{2,5},{3,4},{4,7},{5,6},{6,9},{7,8},{8,11},{9,10},{10,... | collective-permute-start | bytes 1966088 | tf_op jit(solution)/shard_map/ppermute | solution.py:257
  42.6 1.3 slice.12
  45.3 0.9 dynamic-slice_reduce_fusion
  46.2 0.7 reshape.31.two_ref
  47.0 0.7 reshape.30.one_ref
  47.7 5.1 %copy.25 = bf16[1024,4,512]{2,0,1:T(8,128)(2,1)} copy(bf16[1024,4,512]{2,1,0:T(4,128)(2,1)} %param.14) | data formatting | bytes 8388608 | tf_op args[3]
  52.7 2.8 %shard_map.111.refs_6_ = bf16[160,160]{1,0:T(8,128)(2,1)} custom-call(f32[10,160]{1,0:T(8,128)} %reshape.30.one_ref, f32[10,160]{1,0:T(8,128)} %reshape.31.two_ref, bf16[4,160,160]{2,1,0:T(8,128)(2,1)} %constant.32.clone.rows_ref, f32[160,160]{1,0:T(8,128)} %constant.33.clone.match_ref, bf16[4,160,160]{2,1,0:T(8,128)(2,1)} %constant.34.clone.columns_ref), custom_call_target="tpu_custom_call" | custom-call | tf_op jit(solution)/shard_map/pallas_call | solution.py:238
  55.6 0.7 collective-permute-start.8
  56.4 0.7 copy-done.3
  57.1 15.9 %shard_map.112 = bf16[256,1024]{1,0:T(8,128)(2,1)} custom-call(bf16[640,512]{1,0:T(8,128)(2,1)} %copy-done.3, bf16[640,512]{1,0:T(8,128)(2,1)} %copy-done.2, s32[8,128]{1,0:T(8,128)} %shard_map.109.start_ref.refs_2_, s32[200]{0:T(256)} %refs_3_.5, bf16[4,1024,512]{2,1,0:T(8,128)(2,1)} %bitcast.17, bf16[10,1024,512]{2,1,0:T(8,128)(2,1)} %bitcast.24, ...), custom_call_target="tpu_custom_call" | custom-call | flops 8053063680 | bytes 16515072 | tf_op jit(solution)/shard_map/pallas_call | solution.py:188
  73.1 3.2 %collective-permute-start.2 = (bf16[256,1024]{1,0:T(8,128)(2,1)}, bf16[256,1024]{1,0:T(8,128)(2,1)S(1)}, u32[]{:S(2)}, u32[]{:S(2)}) collective-permute-start(bf16[256,1024]{1,0:T(8,128)(2,1)} %shard_map.112), channel_id=1, source_target_pairs={{0,30},{1,31},{2,0},{3,1},{4,2},{5,3},{6,4},{7,5},{8,6},{9,7},{10,... | collective-permute-start | bytes 1572872 | tf_op jit(solution)/shard_map/ppermute | solution.py:257
  76.3 22.1 %shard_map.114 = bf16[512,1024]{1,0:T(8,128)(2,1)} custom-call(bf16[1280,512]{1,0:T(8,128)(2,1)} %collective-permute-done.4.refs_0_, bf16[1280,512]{1,0:T(8,128)(2,1)} %collective-permute-done.5.refs_1_, s32[8,128]{1,0:T(8,128)} %shard_map.109.start_ref.refs_2_, s32[200]{0:T(256)} %refs_3_.5, bf16[4,1024,512]{2,1,0:T(8,128)(2,1)} %bitcast.18, ...), custom_call_target="tpu_custom_call" | custom-call | flops 16106127360 | bytes 18350080 | tf_op jit(solution)/shard_map/pallas_call | solution.py:188
  98.4 1.2 collective-permute-start.7
  99.6 1.0 collective-permute-start.6
  100.6 0.8 copy-done.4
  101.5 15.9 %shard_map.116 = bf16[256,1024]{1,0:T(8,128)(2,1)} custom-call(bf16[640,512]{1,0:T(8,128)(2,1)} %copy-done.4, bf16[640,512]{1,0:T(8,128)(2,1)} %collective-permute-done.9.refs_1_, s32[8,128]{1,0:T(8,128)} %shard_map.109.start_ref.refs_2_, s32[200]{0:T(256)} %refs_3_.5, bf16[4,1024,512]{2,1,0:T(8,128)(2,1)} %bitcast.19, bf16[10,1024,512]{2,1,0:T(8,128)(2,1)} %bitcast.26, ...), custom_call_target="tpu_custom_call" | custom-call | flops 8053063680 | bytes 16515072 | tf_op jit(solution)/shard_map/pallas_call | solution.py:188
  117.8 0.9 collective-permute-start.10
  120.7 13.4 %collective-permute-done.11 = bf16[256,1024]{1,0:T(8,128)(2,1)} collective-permute-done((bf16[256,1024]{1,0:T(8,128)(2,1)}, bf16[256,1024]{1,0:T(8,128)(2,1)}, u32[]{:S(2)}, u32[]{:S(2)}) %collective-permute-start.11) | collective-permute-done | bytes 524320 | tf_op jit(solution)/shard_map/ppermute | solution.py:257
  134.1 2.3 %collective-permute-done.10 = bf16[256,1024]{1,0:T(8,128)(2,1)} collective-permute-done((bf16[256,1024]{1,0:T(8,128)(2,1)}, bf16[256,1024]{1,0:T(8,128)(2,1)}, u32[]{:S(2)}, u32[]{:S(2)}) %collective-permute-start.10) | collective-permute-done | bytes 524320 | tf_op jit(solution)/shard_map/ppermute | solution.py:257
  136.4 1.6 %select_convert_fusion.2 = (bf16[256,1024]{1,0:T(8,128)(2,1)S(1)}, bf16[256,1024]{1,0:T(8,128)(2,1)S(1)}) fusion(bf16[256,1024]{1,0:T(8,128)(2,1)S(1)} %collective-permute-done.3, bf16[256,1024]{1,0:T(8,128)(2,1)S(1)} %collective-permute-done.2, pred[1024]{0:T(1024)(128)(4,1)S(1)} %iota_compare_fusion, bf16[256,1024]{1,0:T(8,128)(2,1)} %collective-permute-done.11, ...), kind=kLoop, calls=%fused_computation.5 | loop fusion | flops 2621440 | bytes 3146752 | tf_op jit(solution)/shard_map/convert_element_type | solution.py:296
  138.7 2.2 %reshape.34 = bf16[64,4,4,1024]{3,2,1,0:T(4,128)(2,1)} reshape(bf16[1024,1024]{1,0:T(8,128)(2,1)S(1)} %pad_maximum_fusion) | data formatting | bytes 4194304 | tf_op jit(solution)/shard_map/reshape | solution.py:297
  (34 shorter events, 4.7 us)
Async XLA Ops:
  18.2 7.8 %slice-start = ((bf16[64,10,1024]{2,0,1:T(8,128)(2,1)}), bf16[32,10,1024]{2,0,1:T(8,128)(2,1)S(1)}, s32[]{:S(2)}) async-start(bf16[64,10,1024]{2,0,1:T(8,128)(2,1)} %param.11), calls=%async_computation | async-start | bytes 1310720 | tf_op jit(solution)/shard_map/slice | solution.py:277
  23.1 32.4 %collective-permute-start.1 = (bf16[640,512]{1,0:T(8,128)(2,1)}, bf16[640,512]{1,0:T(8,128)(2,1)S(1)}, u32[]{:S(2)}, u32[]{:S(2)}) collective-permute-start(bf16[640,512]{1,0:T(8,128)(2,1)} %shard_map.110), channel_id=1, source_target_pairs={{0,3},{1,2},{2,5},{3,4},{4,7},{5,6},{6,9},{7,8},{8,11},{9,10},{10,... | collective-permute-start | bytes 1966088 | tf_op jit(solution)/shard_map/ppermute | solution.py:257
  25.7 30.5 %collective-permute-start = (bf16[640,512]{1,0:T(8,128)(2,1)}, bf16[640,512]{1,0:T(8,128)(2,1)S(1)}, u32[]{:S(2)}, u32[]{:S(2)}) collective-permute-start(bf16[640,512]{1,0:T(8,128)(2,1)} %shard_map.110), channel_id=1, source_target_pairs={{0,2},{1,3},{2,4},{3,5},{4,6},{5,7},{6,8},{7,9},{8,10},{9,11},{10,... | collective-permute-start | bytes 1966088 | tf_op jit(solution)/shard_map/ppermute | solution.py:257
  33.4 39.7 %collective-permute-start.5 = (bf16[1280,512]{1,0:T(8,128)(2,1)}, bf16[1280,512]{1,0:T(8,128)(2,1)}, u32[]{:S(2)}, u32[]{:S(2)}) collective-permute-start(bf16[1280,512]{1,0:T(8,128)(2,1)} %shard_map.113), channel_id=1, source_target_pairs={{0,3},{1,2},{2,5},{3,4},{4,7},{5,6},{6,9},{7,8},{8,11},{9,10},{10,... | collective-permute-start | bytes 3932168 | tf_op jit(solution)/shard_map/ppermute | solution.py:257
  34.1 42.2 %collective-permute-start.4 = (bf16[1280,512]{1,0:T(8,128)(2,1)}, bf16[1280,512]{1,0:T(8,128)(2,1)}, u32[]{:S(2)}, u32[]{:S(2)}) collective-permute-start(bf16[1280,512]{1,0:T(8,128)(2,1)} %shard_map.113), channel_id=1, source_target_pairs={{0,2},{1,3},{2,4},{3,5},{4,6},{5,7},{6,8},{7,9},{8,10},{9,11},{10,... | collective-permute-start | bytes 3932168 | tf_op jit(solution)/shard_map/ppermute | solution.py:257
  40.4 59.2 %collective-permute-start.9 = (bf16[640,512]{1,0:T(8,128)(2,1)}, bf16[640,512]{1,0:T(8,128)(2,1)}, u32[]{:S(2)}, u32[]{:S(2)}) collective-permute-start(bf16[640,512]{1,0:T(8,128)(2,1)} %shard_map.115), channel_id=1, source_target_pairs={{0,3},{1,2},{2,5},{3,4},{4,7},{5,6},{6,9},{7,8},{8,11},{9,10},{10,... | collective-permute-start | bytes 1966088 | tf_op jit(solution)/shard_map/ppermute | solution.py:257
  47.7 7.9 %copy-start = (bf16[640,512]{1,0:T(8,128)(2,1)S(1)}, bf16[640,512]{1,0:T(8,128)(2,1)}, u32[]{:S(2)}) copy-start(bf16[640,512]{1,0:T(8,128)(2,1)} %shard_map.115) | copy-start | bytes 1966084
  55.6 0.9 copy-start.2
  55.6 45.0 %collective-permute-start.8 = (bf16[640,512]{1,0:T(8,128)(2,1)S(1)}, bf16[640,512]{1,0:T(8,128)(2,1)S(1)}, u32[]{:S(2)}, u32[]{:S(2)}) collective-permute-start(bf16[640,512]{1,0:T(8,128)(2,1)S(1)} %copy-done), channel_id=1, source_target_pairs={{0,2},{1,3},{2,4},{3,5},{4,6},{5,7},{6,8},{7,9},{8,10},{9,11},{10,... | collective-permute-start | bytes 1966088 | tf_op jit(solution)/shard_map/ppermute | solution.py:257
  56.2 0.9 copy-start.3
  73.1 44.7 %collective-permute-start.3 = (bf16[256,1024]{1,0:T(8,128)(2,1)}, bf16[256,1024]{1,0:T(8,128)(2,1)S(1)}, u32[]{:S(2)}, u32[]{:S(2)}) collective-permute-start(bf16[256,1024]{1,0:T(8,128)(2,1)} %shard_map.112), channel_id=1, source_target_pairs={{0,31},{1,30},{2,1},{3,0},{4,3},{5,2},{6,5},{7,4},{8,7},{9,6},{10,... | collective-permute-start | bytes 1572872 | tf_op jit(solution)/shard_map/ppermute | solution.py:257
  73.1 47.6 %collective-permute-start.2 = (bf16[256,1024]{1,0:T(8,128)(2,1)}, bf16[256,1024]{1,0:T(8,128)(2,1)S(1)}, u32[]{:S(2)}, u32[]{:S(2)}) collective-permute-start(bf16[256,1024]{1,0:T(8,128)(2,1)} %shard_map.112), channel_id=1, source_target_pairs={{0,30},{1,31},{2,0},{3,1},{4,2},{5,3},{6,4},{7,5},{8,6},{9,7},{10,... | collective-permute-start | bytes 1572872 | tf_op jit(solution)/shard_map/ppermute | solution.py:257
  98.4 21.1 %copy-start.1 = (s32[200]{0:T(256)S(1)}, s32[200]{0:T(256)}, u32[]{:S(2)}) copy-start(s32[200]{0:T(256)} %refs_3_.5) | copy-start | bytes 2404
  98.4 39.7 %collective-permute-start.7 = (bf16[512,1024]{1,0:T(8,128)(2,1)}, bf16[512,1024]{1,0:T(8,128)(2,1)S(1)}, u32[]{:S(2)}, u32[]{:S(2)}) collective-permute-start(bf16[512,1024]{1,0:T(8,128)(2,1)} %shard_map.114), channel_id=1, source_target_pairs={{0,31},{1,30},{2,1},{3,0},{4,3},{5,2},{6,5},{7,4},{8,7},{9,6},{10,... | collective-permute-start | bytes 3145736 | tf_op jit(solution)/shard_map/ppermute | solution.py:257
  99.6 38.5 %collective-permute-start.6 = (bf16[512,1024]{1,0:T(8,128)(2,1)}, bf16[512,1024]{1,0:T(8,128)(2,1)S(1)}, u32[]{:S(2)}, u32[]{:S(2)}) collective-permute-start(bf16[512,1024]{1,0:T(8,128)(2,1)} %shard_map.114), channel_id=1, source_target_pairs={{0,30},{1,31},{2,0},{3,1},{4,2},{5,3},{6,4},{7,5},{8,6},{9,7},{10,... | collective-permute-start | bytes 3145736 | tf_op jit(solution)/shard_map/ppermute | solution.py:257
  100.6 0.8 copy-start.4
  117.4 16.8 %collective-permute-start.11 = (bf16[256,1024]{1,0:T(8,128)(2,1)}, bf16[256,1024]{1,0:T(8,128)(2,1)}, u32[]{:S(2)}, u32[]{:S(2)}) collective-permute-start(bf16[256,1024]{1,0:T(8,128)(2,1)} %shard_map.116), channel_id=1, source_target_pairs={{0,31},{1,30},{2,1},{3,0},{4,3},{5,2},{6,5},{7,4},{8,7},{9,6},{10,... | collective-permute-start | bytes 1572872 | tf_op jit(solution)/shard_map/ppermute | solution.py:257
  117.8 18.6 %collective-permute-start.10 = (bf16[256,1024]{1,0:T(8,128)(2,1)}, bf16[256,1024]{1,0:T(8,128)(2,1)}, u32[]{:S(2)}, u32[]{:S(2)}) collective-permute-start(bf16[256,1024]{1,0:T(8,128)(2,1)} %shard_map.116), channel_id=1, source_target_pairs={{0,30},{1,31},{2,0},{3,1},{4,2},{5,3},{6,4},{7,5},{8,6},{9,7},{10,... | collective-permute-start | bytes 1572872 | tf_op jit(solution)/shard_map/ppermute | solution.py:257

commit v4 on v3

--- a/solution.py
+++ b/solution.py
@@ -126,9 +126,9 @@
 
 def apply_kernel(pieces, *refs):
     rows_refs = refs[:pieces]
-    start_ref, profile_ref, site_ref, env_ref, pair_ref, out_ref, mixed, total = refs[pieces:]
-    step = pl.program_id(0)
-    last = pl.num_programs(0) - 1
+    start_ref, profile_ref, site_ref, env_ref, pair_ref, out_ref, mixed, total, env_held, env_sem = refs[pieces:]
+    env_copy = pltpu.make_async_copy(env_ref, env_held, env_sem)
+    env_copy.start()
     place = lax.axis_index("env")
     states, _, width = site_ref.shape
     block = rows_refs[0].shape[1]
@@ -136,45 +136,45 @@
     pairs = pair_ref.shape[0] // bonds
     tall = pair_ref.shape[1] // states
 
-    @pl.when(step == 0)
-    def _():
-        right_live = profile_ref[lax.rem(start_ref[0, 0], profile_ref.shape[0])]
-        ids = place * width + lax.broadcasted_iota(jnp.int32, (1, width), 1)
-        keep = (ids < right_live).astype(jnp.float32)
-
-        def group(g, carry):
-            base = pl.multiple_of(g * (GROUP * tall), 16)
-            parts = []
-            for v in range(states):
-                term = None
-                for r in range(pieces):
-                    at = pl.multiple_of(lax.rem(place - r + pieces, pieces) * block, 128)
-                    one = jnp.dot(
-                        rows_refs[r][pl.ds(base, GROUP * tall), :],
-                        site_ref[v, pl.ds(at, block), :],
-                        preferred_element_type=jnp.float32,
-                    )
-                    term = one if term is None else term + one
-                parts.append(term * keep)
-            for i in range(GROUP):
-                inner = jnp.concatenate([p[i * tall:(i + 1) * tall] for p in parts], axis=0)
-                out = jnp.dot(pair_ref[...], inner.astype(jnp.bfloat16), preferred_element_type=jnp.float32)
-                out = out.astype(jnp.bfloat16)
-                start = pl.multiple_of((g * GROUP + i) * pairs, 16)
-                for k in range(bonds):
-                    mixed[k, pl.ds(start, pairs), :] = out[k * pairs:(k + 1) * pairs]
-            return carry
-
-        lax.fori_loop(0, mixed.shape[1] // (GROUP * pairs), group, 0)
-        total[...] = jnp.zeros_like(total)
-
-    total[...] += lax.dot_general(
-        mixed[step], env_ref[0], (((1,), (1,)), ((), ())), preferred_element_type=jnp.float32
-    )
-
-    @pl.when(step == last)
-    def _():
-        out_ref[...] = total[...].astype(out_ref.dtype)
+    right_live = profile_ref[lax.rem(start_ref[0, 0], profile_ref.shape[0])]
+    ids = place * width + lax.broadcasted_iota(jnp.int32, (1, width), 1)
+    keep = (ids < right_live).astype(jnp.float32)
+
+    def group(g, carry):
+        base = pl.multiple_of(g * (GROUP * tall), 16)
+        parts = []
+        for v in range(states):
+            term = None
+            for r in range(pieces):
+                at = pl.multiple_of(lax.rem(place - r + pieces, pieces) * block, 128)
+                one = jnp.dot(
+                    rows_refs[r][pl.ds(base, GROUP * tall), :],
+                    site_ref[v, pl.ds(at, block), :],
+                    preferred_element_type=jnp.float32,
+                )
+                term = one if term is None else term + one
+            parts.append(term * keep)
+        for i in range(GROUP):
+            inner = jnp.concatenate([p[i * tall:(i + 1) * tall] for p in parts], axis=0)
+            out = jnp.dot(pair_ref[...], inner.astype(jnp.bfloat16), preferred_element_type=jnp.float32)
+            out = out.astype(jnp.bfloat16)
+            start = pl.multiple_of((g * GROUP + i) * pairs, 16)
+            for k in range(bonds):
+                mixed[k, pl.ds(start, pairs), :] = out[k * pairs:(k + 1) * pairs]
+        return carry
+
+    lax.fori_loop(0, mixed.shape[1] // (GROUP * pairs), group, 0)
+    total[...] = jnp.zeros_like(total)
+    env_copy.wait()
+
+    def bond(k, carry):
+        total[...] += lax.dot_general(
+            mixed[k], env_held[k], (((1,), (1,)), ((), ())), preferred_element_type=jnp.float32
+        )
+        return carry
+
+    lax.fori_loop(0, bonds, bond, 0)
+    out_ref[...] = total[...].astype(out_ref.dtype)
 
 
 def make_terms(rows_pieces, start, profile, site, env, pair):
@@ -184,23 +184,18 @@
     bonds, outs, _ = env.shape
     tall = bonds * states
     lines = count // tall * states * states
-    whole = lambda k: (0, 0)
+    near = pl.BlockSpec(memory_space=pltpu.VMEM)
+    table = pl.BlockSpec(memory_space=pltpu.SMEM)
     return pl.pallas_call(
         functools.partial(apply_kernel, pieces),
-        grid=(bonds,),
-        in_specs=[pl.BlockSpec((count, block), whole)] * pieces
-        + [
-            pl.BlockSpec(memory_space=pltpu.SMEM),
-            pl.BlockSpec(memory_space=pltpu.SMEM),
-            pl.BlockSpec((states, depth, width), lambda k: (0, 0, 0)),
-            pl.BlockSpec((1, outs, width), lambda k: (k, 0, 0)),
-            pl.BlockSpec(pair.shape, whole),
-        ],
-        out_specs=pl.BlockSpec((lines, outs), whole),
+        in_specs=[near] * pieces + [table, table, near, pl.BlockSpec(memory_space=pl.ANY), near],
+        out_specs=near,
         out_shape=jax.ShapeDtypeStruct((lines, outs), jnp.bfloat16),
         scratch_shapes=[
             pltpu.VMEM((bonds, lines, width), jnp.bfloat16),
             pltpu.VMEM((lines, outs), jnp.float32),
+            pltpu.VMEM(env.shape, jnp.bfloat16),
+            pltpu.SemaphoreType.DMA,
         ],
         compiler_params=pltpu.CompilerParams(vmem_limit_bytes=VMEM_BYTES),
         cost_estimate=pl.CostEstimate(

time: 142 us -> 156 us (1.099)
  waiting for transfers between devices: 15.7 us -> 35.4 us
  Pallas kernels: 82.2 us -> 71.9 us
  starting transfers between devices: 13.6 us -> 18.2 us
    ppermute x12, waiting for transfers between devices: 15.7 us -> 35.4 us  [hop(): return lax.ppermute(value, ('sec', 'env'), pairs)]
    pallas_call x3, Pallas kernels: 54 us -> 43.7 us  [make_terms(): pl.pallas_call(functools.partial(apply_kernel, pieces), in_specs=[near] *...]
    ppermute x12, starting transfers between devices: 13.6 us -> 18.2 us  [hop(): return lax.ppermute(value, ('sec', 'env'), pairs)]
  transfers between devices with their start and end apart: 12 -> 12, of which waited for: 2 -> 2; matrix products, arithmetic and copies ran while one was open for 10% -> 9% of each run, Pallas kernels for 48% -> 37%
where the time goes in v4:
time: 156 us; the launch traced here: 155 us
  Pallas kernels  71.9 us (46%)
  waiting for transfers between devices  35.4 us (23%)
  local copies, waits for them, and re-layouts  23.5 us (15%)
  starting transfers between devices  18.2 us (12%)
  between operations  2.98 us (2%)
  other arithmetic  2.86 us (2%)
    pallas_call x3, Pallas kernels, make_terms(): pl.pallas_call(functools.partial(apply_kernel, pieces), in_specs=[near] *...  43.7 us
    ppermute x12, waiting for transfers between devices, hop(): return lax.ppermute(value, ('sec', 'env'), pairs)  35.4 us
    ppermute x12, starting transfers between devices, hop(): return lax.ppermute(value, ('sec', 'env'), pairs)  18.2 us
    pallas_call x3, Pallas kernels, make_rows(): pl.pallas_call(row_kernel, grid=(states,), in_specs=[pl.BlockSpec(memory_...  15.6 us
    unnamed x12, local copies, waits for them, and re-layouts  11.8 us
    pallas_call x1, Pallas kernels, earlier_sites(): pl.pallas_call(count_kernel, in_specs=[pl.BlockSpec(memory_space=pltpu.VM...  9.78 us
  transfers between devices with their start and end apart: 12, of which 2 were waited for; matrix products, arithmetic and copies ran while one was open for 9% of the time, Pallas kernels for 37%

profile of v4, /device:TPU:1, one launch (start us, length us, event | category | flops | bytes accessed | tf_op | source)
XLA Modules:
  0.0 154.9 jit_solution(538624189796323022)
XLA Ops:
  1.2 9.8 %shard_map.109.start_ref.refs_2_ = s32[8,128]{1,0:T(8,128)} custom-call(s32[8,128]{1,0:T(8,128)} %broadcast_in_dim.41.length_ref), custom_call_target="tpu_custom_call" | custom-call | tf_op jit(solution)/shard_map/pallas_call | solution.py:50
  11.0 1.1 fusion
  12.4 0.8 reshape.28.env_ref
  13.2 5.0 %copy.26 = bf16[1024,4,512]{2,0,1:T(8,128)(2,1)} copy(bf16[1024,4,512]{2,1,0:T(4,128)(2,1)} %param.12) | data formatting | bytes 8388608 | tf_op args[1]
  18.2 4.9 %shard_map.110 = bf16[640,512]{1,0:T(8,128)(2,1)} custom-call(s32[8,128]{1,0:T(8,128)} %shard_map.109.start_ref.refs_2_, s32[1]{0:T(128)} %copy.27.length_ref, s32[200]{0:T(256)} %refs_3_.5, bf16[160,1024]{1,0:T(8,128)(2,1)} %reshape.28.env_ref, bf16[4,1024,512]{2,1,0:T(8,128)(2,1)} %bitcast.14, f32[1,512]{1,0:T(1,128)} %bitcast.21), custom_call_target="tpu_custom_call" | custom-call | flops 671088640 | bytes 5177344 | tf_op jit(solution)/shard_map/pallas_call | solution.py:101
  23.1 2.6 %collective-permute-start.1 = (bf16[640,512]{1,0:T(8,128)(2,1)}, bf16[640,512]{1,0:T(8,128)(2,1)S(1)}, u32[]{:S(2)}, u32[]{:S(2)}) collective-permute-start(bf16[640,512]{1,0:T(8,128)(2,1)} %shard_map.110), channel_id=1, source_target_pairs={{0,3},{1,2},{2,5},{3,4},{4,7},{5,6},{6,9},{7,8},{8,11},{9,10},{10,... | collective-permute-start | bytes 1966088 | tf_op jit(solution)/shard_map/ppermute | solution.py:252
  26.4 1.1 reshape.32.env_ref
  27.5 5.9 %shard_map.113 = bf16[1280,512]{1,0:T(8,128)(2,1)} custom-call(s32[8,128]{1,0:T(8,128)} %shard_map.109.start_ref.refs_2_, s32[1]{0:T(128)} %copy.27.length_ref, s32[200]{0:T(256)} %refs_3_.5, bf16[320,1024]{1,0:T(8,128)(2,1)} %reshape.32.env_ref, bf16[4,1024,512]{2,1,0:T(8,128)(2,1)} %bitcast.15, f32[1,512]{1,0:T(1,128)} %bitcast.22), custom_call_target="tpu_custom_call" | custom-call | flops 1342177280 | bytes 6160384 | tf_op jit(solution)/shard_map/pallas_call | solution.py:101
  33.4 0.7 collective-permute-start.5
  34.7 0.9 reshape.33.env_ref
  35.6 4.8 %shard_map.115 = bf16[640,512]{1,0:T(8,128)(2,1)} custom-call(s32[8,128]{1,0:T(8,128)} %shard_map.109.start_ref.refs_2_, s32[1]{0:T(128)} %copy.27.length_ref, s32[200]{0:T(256)} %refs_3_.5, bf16[160,1024]{1,0:T(8,128)(2,1)} %reshape.33.env_ref, bf16[4,1024,512]{2,1,0:T(8,128)(2,1)} %bitcast.16, f32[1,512]{1,0:T(1,128)} %bitcast.23), custom_call_target="tpu_custom_call" | custom-call | flops 671088640 | bytes 5177344 | tf_op jit(solution)/shard_map/pallas_call | solution.py:101
  40.4 2.2 %collective-permute-start.9 = (bf16[640,512]{1,0:T(8,128)(2,1)}, bf16[640,512]{1,0:T(8,128)(2,1)}, u32[]{:S(2)}, u32[]{:S(2)}) collective-permute-start(bf16[640,512]{1,0:T(8,128)(2,1)} %shard_map.115), channel_id=1, source_target_pairs={{0,3},{1,2},{2,5},{3,4},{4,7},{5,6},{6,9},{7,8},{8,11},{9,10},{10,... | collective-permute-start | bytes 1966088 | tf_op jit(solution)/shard_map/ppermute | solution.py:252
  42.6 1.3 slice.12
  45.3 0.9 dynamic-slice_reduce_fusion
  46.1 0.7 reshape.31.two_ref
  46.9 0.7 reshape.30.one_ref
  47.6 5.1 %copy.25 = bf16[1024,4,512]{2,0,1:T(8,128)(2,1)} copy(bf16[1024,4,512]{2,1,0:T(4,128)(2,1)} %param.14) | data formatting | bytes 8388608 | tf_op args[3]
  52.7 2.8 %shard_map.111.refs_6_ = bf16[160,160]{1,0:T(8,128)(2,1)} custom-call(f32[10,160]{1,0:T(8,128)} %reshape.30.one_ref, f32[10,160]{1,0:T(8,128)} %reshape.31.two_ref, bf16[4,160,160]{2,1,0:T(8,128)(2,1)} %constant.32.clone.rows_ref, f32[160,160]{1,0:T(8,128)} %constant.33.clone.match_ref, bf16[4,160,160]{2,1,0:T(8,128)(2,1)} %constant.34.clone.columns_ref), custom_call_target="tpu_custom_call" | custom-call | tf_op jit(solution)/shard_map/pallas_call | solution.py:233
  55.5 0.7 collective-permute-start.8
  56.4 0.7 copy-done.3
  57.1 12.2 %shard_map.112 = bf16[256,1024]{1,0:T(8,128)(2,1)} custom-call(bf16[640,512]{1,0:T(8,128)(2,1)} %copy-done.3, bf16[640,512]{1,0:T(8,128)(2,1)} %copy-done.2, s32[8,128]{1,0:T(8,128)} %shard_map.109.start_ref.refs_2_, s32[200]{0:T(256)} %refs_3_.5, bf16[4,1024,512]{2,1,0:T(8,128)(2,1)} %bitcast.17, bf16[10,1024,512]{2,1,0:T(8,128)(2,1)} %bitcast.24, ...), custom_call_target="tpu_custom_call" | custom-call | flops 8053063680 | bytes 16515072 | tf_op jit(solution)/shard_map/pallas_call | solution.py:189
  69.4 3.2 %collective-permute-start.2 = (bf16[256,1024]{1,0:T(8,128)(2,1)}, bf16[256,1024]{1,0:T(8,128)(2,1)S(1)}, u32[]{:S(2)}, u32[]{:S(2)}) collective-permute-start(bf16[256,1024]{1,0:T(8,128)(2,1)} %shard_map.112), channel_id=1, source_target_pairs={{0,30},{1,31},{2,0},{3,1},{4,2},{5,3},{6,4},{7,5},{8,6},{9,7},{10,... | collective-permute-start | bytes 1572872 | tf_op jit(solution)/shard_map/ppermute | solution.py:252
  72.6 19.4 %shard_map.114 = bf16[512,1024]{1,0:T(8,128)(2,1)} custom-call(bf16[1280,512]{1,0:T(8,128)(2,1)} %collective-permute-done.4.refs_0_, bf16[1280,512]{1,0:T(8,128)(2,1)} %collective-permute-done.5.refs_1_, s32[8,128]{1,0:T(8,128)} %shard_map.109.start_ref.refs_2_, s32[200]{0:T(256)} %refs_3_.5, bf16[4,1024,512]{2,1,0:T(8,128)(2,1)} %bitcast.18, ...), custom_call_target="tpu_custom_call" | custom-call | flops 16106127360 | bytes 18350080 | tf_op jit(solution)/shard_map/pallas_call | solution.py:189
  92.0 1.5 collective-permute-start.7
  93.5 0.7 collective-permute-start.6
  94.2 0.8 copy-done.4
  95.0 12.2 %shard_map.116 = bf16[256,1024]{1,0:T(8,128)(2,1)} custom-call(bf16[640,512]{1,0:T(8,128)(2,1)} %copy-done.4, bf16[640,512]{1,0:T(8,128)(2,1)} %collective-permute-done.9.refs_1_, s32[8,128]{1,0:T(8,128)} %shard_map.109.start_ref.refs_2_, s32[200]{0:T(256)} %refs_3_.5, bf16[4,1024,512]{2,1,0:T(8,128)(2,1)} %bitcast.19, bf16[10,1024,512]{2,1,0:T(8,128)(2,1)} %bitcast.26, ...), custom_call_target="tpu_custom_call" | custom-call | flops 8053063680 | bytes 16515072 | tf_op jit(solution)/shard_map/pallas_call | solution.py:189
  107.2 5.9 %collective-permute-start.11 = (bf16[256,1024]{1,0:T(8,128)(2,1)}, bf16[256,1024]{1,0:T(8,128)(2,1)}, u32[]{:S(2)}, u32[]{:S(2)}) collective-permute-start(bf16[256,1024]{1,0:T(8,128)(2,1)} %shard_map.116), channel_id=1, source_target_pairs={{0,31},{1,30},{2,1},{3,0},{4,3},{5,2},{6,5},{7,4},{8,7},{9,6},{10,... | collective-permute-start | bytes 1572872 | tf_op jit(solution)/shard_map/ppermute | solution.py:252
  115.1 29.7 %collective-permute-done.11 = bf16[256,1024]{1,0:T(8,128)(2,1)} collective-permute-done((bf16[256,1024]{1,0:T(8,128)(2,1)}, bf16[256,1024]{1,0:T(8,128)(2,1)}, u32[]{:S(2)}, u32[]{:S(2)}) %collective-permute-start.11) | collective-permute-done | bytes 524320 | tf_op jit(solution)/shard_map/ppermute | solution.py:252
  144.8 5.7 %collective-permute-done.10 = bf16[256,1024]{1,0:T(8,128)(2,1)} collective-permute-done((bf16[256,1024]{1,0:T(8,128)(2,1)}, bf16[256,1024]{1,0:T(8,128)(2,1)}, u32[]{:S(2)}, u32[]{:S(2)}) %collective-permute-start.10) | collective-permute-done | bytes 524320 | tf_op jit(solution)/shard_map/ppermute | solution.py:252
  150.5 1.6 %select_convert_fusion.2 = (bf16[256,1024]{1,0:T(8,128)(2,1)S(1)}, bf16[256,1024]{1,0:T(8,128)(2,1)S(1)}) fusion(bf16[256,1024]{1,0:T(8,128)(2,1)S(1)} %collective-permute-done.3, bf16[256,1024]{1,0:T(8,128)(2,1)S(1)} %collective-permute-done.2, pred[1024]{0:T(1024)(128)(4,1)S(1)} %iota_compare_fusion, bf16[256,1024]{1,0:T(8,128)(2,1)} %collective-permute-done.11, ...), kind=kLoop, calls=%fused_computation.5 | loop fusion | flops 2621440 | bytes 3146752 | tf_op jit(solution)/shard_map/convert_element_type | solution.py:291
  152.7 2.2 %reshape.34 = bf16[64,4,4,1024]{3,2,1,0:T(4,128)(2,1)} reshape(bf16[1024,1024]{1,0:T(8,128)(2,1)S(1)} %pad_maximum_fusion) | data formatting | bytes 4194304 | tf_op jit(solution)/shard_map/reshape | solution.py:292
  (34 shorter events, 4.3 us)
Async XLA Ops:
  18.2 7.8 %slice-start = ((bf16[64,10,1024]{2,0,1:T(8,128)(2,1)}), bf16[32,10,1024]{2,0,1:T(8,128)(2,1)S(1)}, s32[]{:S(2)}) async-start(bf16[64,10,1024]{2,0,1:T(8,128)(2,1)} %param.11), calls=%async_computation | async-start | bytes 1310720 | tf_op jit(solution)/shard_map/slice | solution.py:272
  23.1 32.4 %collective-permute-start.1 = (bf16[640,512]{1,0:T(8,128)(2,1)}, bf16[640,512]{1,0:T(8,128)(2,1)S(1)}, u32[]{:S(2)}, u32[]{:S(2)}) collective-permute-start(bf16[640,512]{1,0:T(8,128)(2,1)} %shard_map.110), channel_id=1, source_target_pairs={{0,3},{1,2},{2,5},{3,4},{4,7},{5,6},{6,9},{7,8},{8,11},{9,10},{10,... | collective-permute-start | bytes 1966088 | tf_op jit(solution)/shard_map/ppermute | solution.py:252
  25.7 30.5 %collective-permute-start = (bf16[640,512]{1,0:T(8,128)(2,1)}, bf16[640,512]{1,0:T(8,128)(2,1)S(1)}, u32[]{:S(2)}, u32[]{:S(2)}) collective-permute-start(bf16[640,512]{1,0:T(8,128)(2,1)} %shard_map.110), channel_id=1, source_target_pairs={{0,2},{1,3},{2,4},{3,5},{4,6},{5,7},{6,8},{7,9},{8,10},{9,11},{10,... | collective-permute-start | bytes 1966088 | tf_op jit(solution)/shard_map/ppermute | solution.py:252
  33.4 36.0 %collective-permute-start.5 = (bf16[1280,512]{1,0:T(8,128)(2,1)}, bf16[1280,512]{1,0:T(8,128)(2,1)}, u32[]{:S(2)}, u32[]{:S(2)}) collective-permute-start(bf16[1280,512]{1,0:T(8,128)(2,1)} %shard_map.113), channel_id=1, source_target_pairs={{0,3},{1,2},{2,5},{3,4},{4,7},{5,6},{6,9},{7,8},{8,11},{9,10},{10,... | collective-permute-start | bytes 3932168 | tf_op jit(solution)/shard_map/ppermute | solution.py:252
  34.1 38.5 %collective-permute-start.4 = (bf16[1280,512]{1,0:T(8,128)(2,1)}, bf16[1280,512]{1,0:T(8,128)(2,1)}, u32[]{:S(2)}, u32[]{:S(2)}) collective-permute-start(bf16[1280,512]{1,0:T(8,128)(2,1)} %shard_map.113), channel_id=1, source_target_pairs={{0,2},{1,3},{2,4},{3,5},{4,6},{5,7},{6,8},{7,9},{8,10},{9,11},{10,... | collective-permute-start | bytes 3932168 | tf_op jit(solution)/shard_map/ppermute | solution.py:252
  40.4 53.1 %collective-permute-start.9 = (bf16[640,512]{1,0:T(8,128)(2,1)}, bf16[640,512]{1,0:T(8,128)(2,1)}, u32[]{:S(2)}, u32[]{:S(2)}) collective-permute-start(bf16[640,512]{1,0:T(8,128)(2,1)} %shard_map.115), channel_id=1, source_target_pairs={{0,3},{1,2},{2,5},{3,4},{4,7},{5,6},{6,9},{7,8},{8,11},{9,10},{10,... | collective-permute-start | bytes 1966088 | tf_op jit(solution)/shard_map/ppermute | solution.py:252
  47.6 7.9 %copy-start = (bf16[640,512]{1,0:T(8,128)(2,1)S(1)}, bf16[640,512]{1,0:T(8,128)(2,1)}, u32[]{:S(2)}) copy-start(bf16[640,512]{1,0:T(8,128)(2,1)} %shard_map.115) | copy-start | bytes 1966084
  55.5 0.9 copy-start.2
  55.5 38.7 %collective-permute-start.8 = (bf16[640,512]{1,0:T(8,128)(2,1)S(1)}, bf16[640,512]{1,0:T(8,128)(2,1)S(1)}, u32[]{:S(2)}, u32[]{:S(2)}) collective-permute-start(bf16[640,512]{1,0:T(8,128)(2,1)S(1)} %copy-done), channel_id=1, source_target_pairs={{0,2},{1,3},{2,4},{3,5},{4,6},{5,7},{6,8},{7,9},{8,10},{9,11},{10,... | collective-permute-start | bytes 1966088 | tf_op jit(solution)/shard_map/ppermute | solution.py:252
  56.2 0.9 copy-start.3
  69.3 43.8 %collective-permute-start.3 = (bf16[256,1024]{1,0:T(8,128)(2,1)}, bf16[256,1024]{1,0:T(8,128)(2,1)S(1)}, u32[]{:S(2)}, u32[]{:S(2)}) collective-permute-start(bf16[256,1024]{1,0:T(8,128)(2,1)} %shard_map.112), channel_id=1, source_target_pairs={{0,31},{1,30},{2,1},{3,0},{4,3},{5,2},{6,5},{7,4},{8,7},{9,6},{10,... | collective-permute-start | bytes 1572872 | tf_op jit(solution)/shard_map/ppermute | solution.py:252
  69.4 45.7 %collective-permute-start.2 = (bf16[256,1024]{1,0:T(8,128)(2,1)}, bf16[256,1024]{1,0:T(8,128)(2,1)S(1)}, u32[]{:S(2)}, u32[]{:S(2)}) collective-permute-start(bf16[256,1024]{1,0:T(8,128)(2,1)} %shard_map.112), channel_id=1, source_target_pairs={{0,30},{1,31},{2,0},{3,1},{4,2},{5,3},{6,4},{7,5},{8,6},{9,7},{10,... | collective-permute-start | bytes 1572872 | tf_op jit(solution)/shard_map/ppermute | solution.py:252
  91.9 21.9 %copy-start.1 = (s32[200]{0:T(256)S(1)}, s32[200]{0:T(256)}, u32[]{:S(2)}) copy-start(s32[200]{0:T(256)} %refs_3_.5) | copy-start | bytes 2404
  92.0 60.2 %collective-permute-start.7 = (bf16[512,1024]{1,0:T(8,128)(2,1)}, bf16[512,1024]{1,0:T(8,128)(2,1)S(1)}, u32[]{:S(2)}, u32[]{:S(2)}) collective-permute-start(bf16[512,1024]{1,0:T(8,128)(2,1)} %shard_map.114), channel_id=1, source_target_pairs={{0,31},{1,30},{2,1},{3,0},{4,3},{5,2},{6,5},{7,4},{8,7},{9,6},{10,... | collective-permute-start | bytes 3145736 | tf_op jit(solution)/shard_map/ppermute | solution.py:252
  93.5 58.6 %collective-permute-start.6 = (bf16[512,1024]{1,0:T(8,128)(2,1)}, bf16[512,1024]{1,0:T(8,128)(2,1)S(1)}, u32[]{:S(2)}, u32[]{:S(2)}) collective-permute-start(bf16[512,1024]{1,0:T(8,128)(2,1)} %shard_map.114), channel_id=1, source_target_pairs={{0,30},{1,31},{2,0},{3,1},{4,2},{5,3},{6,4},{7,5},{8,6},{9,7},{10,... | collective-permute-start | bytes 3145736 | tf_op jit(solution)/shard_map/ppermute | solution.py:252
  94.2 0.8 copy-start.4
  107.2 37.6 %collective-permute-start.11 = (bf16[256,1024]{1,0:T(8,128)(2,1)}, bf16[256,1024]{1,0:T(8,128)(2,1)}, u32[]{:S(2)}, u32[]{:S(2)}) collective-permute-start(bf16[256,1024]{1,0:T(8,128)(2,1)} %shard_map.116), channel_id=1, source_target_pairs={{0,31},{1,30},{2,1},{3,0},{4,3},{5,2},{6,5},{7,4},{8,7},{9,6},{10,... | collective-permute-start | bytes 1572872 | tf_op jit(solution)/shard_map/ppermute | solution.py:252
  113.1 37.4 %collective-permute-start.10 = (bf16[256,1024]{1,0:T(8,128)(2,1)}, bf16[256,1024]{1,0:T(8,128)(2,1)}, u32[]{:S(2)}, u32[]{:S(2)}) collective-permute-start(bf16[256,1024]{1,0:T(8,128)(2,1)} %shard_map.116), channel_id=1, source_target_pairs={{0,30},{1,31},{2,0},{3,1},{4,2},{5,3},{6,4},{7,5},{8,6},{9,7},{10,... | collective-permute-start | bytes 1572872 | tf_op jit(solution)/shard_map/ppermute | solution.py:252
